TPU v7x, 128 devices: a whole 4x4x4 slice. The times are simulated.
128 devices in a mesh: lon: 8 (over x, core), lat: 16 (over y, z).
Axes of the slice: x: 4, y: 4, z: 4, core: 2. Of those that a mesh axis runs over, the one named last changes fastest.
Arguments:
- radiances: bfloat16 [262144, 128], P(('lon', 'lat')), may hold values from -6 to 6
- block_tile: int32 [2048], P(('lon', 'lat')), may hold values from 0 to 15, as said below
- block_rows: int32 [2048], P(('lon', 'lat')), may hold values from 1 to 128
- row_cells: int32 [262144], P(('lon', 'lat')), may hold values from 0 to 511
- latents: bfloat16 [64, 1024, 1024], P('lat', 'lon'), may hold values from -6 to 6
- disk_pixels: bfloat16 [5, 16, 64, 1024], P(None, None, 'lat', 'lon'), may hold values from -6 to 6
- targets: float32 [64, 1024, 128], P('lat', 'lon'), may hold values from -6 to 6
- w_query: bfloat16 [1024, 1024], replicated, may hold values from -0.1875 to 0.1875
- w_key: bfloat16 [128, 1024], replicated, may hold values from -0.5 to 0.5
- w_value: bfloat16 [128, 1024], replicated, may hold values from -0.5 to 0.5
- w_disk_key: bfloat16 [16, 1024], replicated, may hold values from -1.5 to 1.5
- w_disk_value: bfloat16 [16, 1024], replicated, may hold values from -1.5 to 1.5
- w_out: bfloat16 [1024, 1024], replicated, may hold values from -0.1875 to 0.1875
- w_decode: bfloat16 [1024, 128], replicated, may hold values from -0.1875 to 0.1875
Outputs:
- total_loss: float32 [], replicated
- latent_grad: float32 [64, 1024, 1024], P('lat', 'lon')
- row_grad: bfloat16 [262144, 128], P(('lon', 'lat'))
- update_query: float32 [1024, 1024], P(('lon', 'lat'))
- update_out: float32 [1024, 1024], P(('lon', 'lat'))
- update_key: float32 [128, 1024], replicated
- update_value: float32 [128, 1024], replicated
- update_disk_key: float32 [16, 1024], replicated
- update_disk_value: float32 [16, 1024], replicated
Inputs may be any that keep to these rules, and one draw needn't show every extreme that they name: `block_tile`: tile index within the reading device's longitude column. A device sends at most 2 of its 16 blocks to one tile; in every longitude column one tile gets exactly 2 blocks from every device of that column. `row_cells`: cell numbered row-major over 4 grid rows of 128 columns of the tile.
All inputs are finite; a program needn't handle non-finite values.
Results may differ from a plain program's by a relative error of at most 0.019.
Values may be sent and summed in bfloat16 or wider, within the bound.
A program may use at most 128 MiB of HBM per device.

v0:
```python
import math

import jax
import jax.numpy as jnp
from jax import lax
from jax.sharding import PartitionSpec as P

HEADS = 16
CAP = 2


def latitude_weights(row_total):
    centres = (jnp.arange(row_total, dtype=jnp.float32) + 0.5) / row_total
    return jnp.cos(math.pi / 180.0 * (-60.0 + 120.0 * centres))


def head_sums(product, head_count):
    return jnp.sum(product.reshape(product.shape[0], head_count, -1), axis=2)


def per_head(head_weights, values):
    head_count = head_weights.shape[1]
    spread = head_weights[:, :, None] * values.reshape(values.shape[0], head_count, -1)
    return spread.reshape(values.shape)


def normalized(gradient):
    return gradient / jnp.sqrt(jnp.mean(gradient * gradient) + 1e-06)


def row_forward(query_low, w_key, w_value, row_feats, row_cell, row_valid, head_count, score_scale):
    key_rows = jnp.dot(row_feats, w_key, preferred_element_type=jnp.float32)
    value_rows = jnp.dot(row_feats, w_value, preferred_element_type=jnp.float32)
    query_rows = query_low[row_cell].astype(jnp.float32)
    gating = (
        jax.nn.sigmoid(head_sums(query_rows * key_rows, head_count) * score_scale)
        * row_valid[:, None]
    )
    return per_head(gating, value_rows)


def row_backward(
    query_low, w_key, w_value, grad_mixed, row_feats, row_cell, row_valid, head_count, score_scale
):
    key_rows = jnp.dot(row_feats, w_key, preferred_element_type=jnp.float32)
    value_rows = jnp.dot(row_feats, w_value, preferred_element_type=jnp.float32)
    query_rows = query_low[row_cell].astype(jnp.float32)
    gating = (
        jax.nn.sigmoid(head_sums(query_rows * key_rows, head_count) * score_scale)
        * row_valid[:, None]
    )
    grad_rows = grad_mixed[row_cell]
    grad_value = per_head(gating, grad_rows).astype(jnp.bfloat16)
    grad_score = (
        head_sums(grad_rows * value_rows, head_count) * gating * (1.0 - gating) * score_scale
    )
    grad_key = per_head(grad_score, query_rows).astype(jnp.bfloat16)
    query_term = per_head(grad_score, key_rows)
    grad_wkey = jnp.dot(row_feats.T, grad_key, preferred_element_type=jnp.float32)
    grad_wvalue = jnp.dot(row_feats.T, grad_value, preferred_element_type=jnp.float32)
    back_key = jnp.dot(grad_key, w_key.T, preferred_element_type=jnp.float32)
    back_value = jnp.dot(grad_value, w_value.T, preferred_element_type=jnp.float32)
    return (query_term, grad_wkey, grad_wvalue, (back_key + back_value).astype(jnp.bfloat16))


def disk_forward(query_low, disk_flat, w_disk_key, w_disk_value, head_count, score_scale):
    query_full = query_low.astype(jnp.float32)

    def one_disk(running_sum, pixels):
        disk_key = jnp.dot(pixels.T, w_disk_key, preferred_element_type=jnp.float32)
        disk_value = jnp.dot(pixels.T, w_disk_value, preferred_element_type=jnp.float32)
        gating = jax.nn.sigmoid(head_sums(query_full * disk_key, head_count) * score_scale)
        return (running_sum + per_head(gating, disk_value), None)

    result, unused = lax.scan(one_disk, jnp.zeros(query_low.shape, jnp.float32), disk_flat)
    return result


def disk_backward(
    query_low, disk_flat, w_disk_key, w_disk_value, grad_mixed, head_count, score_scale
):
    query_full = query_low.astype(jnp.float32)

    def one_disk(carried, pixels):
        grad_query, grad_wkey, grad_wvalue = carried
        disk_key = jnp.dot(pixels.T, w_disk_key, preferred_element_type=jnp.float32)
        disk_value = jnp.dot(pixels.T, w_disk_value, preferred_element_type=jnp.float32)
        gating = jax.nn.sigmoid(head_sums(query_full * disk_key, head_count) * score_scale)
        grad_value = per_head(gating, grad_mixed).astype(jnp.bfloat16)
        grad_score = (
            head_sums(grad_mixed * disk_value, head_count) * gating * (1.0 - gating) * score_scale
        )
        grad_key = per_head(grad_score, query_full).astype(jnp.bfloat16)
        grad_query = grad_query + per_head(grad_score, disk_key)
        grad_wkey = grad_wkey + jnp.dot(pixels, grad_key, preferred_element_type=jnp.float32)
        grad_wvalue = grad_wvalue + jnp.dot(pixels, grad_value, preferred_element_type=jnp.float32)
        return ((grad_query, grad_wkey, grad_wvalue), None)

    start_state = (
        jnp.zeros(query_low.shape, jnp.float32),
        jnp.zeros(w_disk_key.shape, jnp.float32),
        jnp.zeros(w_disk_value.shape, jnp.float32),
    )
    result, unused = lax.scan(one_disk, start_state, disk_flat)
    return result


def body(
    radiances,
    block_tile,
    block_rows,
    row_cells,
    latents,
    disk_pixels,
    targets,
    w_query,
    w_key,
    w_value,
    w_disk_key,
    w_disk_value,
    w_out,
    w_decode,
):
    lat_count = lax.axis_size("lat")
    device_count = lax.axis_size(("lon", "lat"))
    block_count = block_tile.shape[0]
    block_len = radiances.shape[0] // block_count
    feat_width = radiances.shape[1]
    tile_lat, tile_lon, model_width = latents.shape
    out_width = targets.shape[2]
    cell_count = tile_lat * tile_lon
    head_count = HEADS
    score_scale = 1.0 / math.sqrt(model_width // head_count)
    capacity = CAP
    slot_count = lat_count * capacity
    earlier = jnp.tril((block_tile[:, None] == block_tile[None, :]).astype(jnp.int32), -1)
    slot_of_block = block_tile * capacity + jnp.sum(earlier, axis=1)
    slot_match = (
        slot_of_block[None, :] == jnp.arange(slot_count, dtype=jnp.int32)[:, None]
    ).astype(jnp.int32)
    filled = jnp.sum(slot_match, axis=1)
    source = jnp.sum(slot_match * jnp.arange(block_count, dtype=jnp.int32)[None, :], axis=1)
    blocks = radiances.reshape(block_count, block_len, feat_width)
    send_feats = (blocks[source] * filled[:, None, None].astype(jnp.bfloat16)).reshape(
        lat_count, capacity, block_len, feat_width
    )
    send_cells = row_cells.reshape(block_count, block_len)[source].reshape(
        lat_count, capacity, block_len
    )
    send_rows = (block_rows[source] * filled).reshape(lat_count, capacity)
    got_feats, got_cells, got_rows = (
        lax.all_to_all(send_feats, "lat", split_axis=0, concat_axis=0, tiled=True),
        lax.all_to_all(send_cells, "lat", split_axis=0, concat_axis=0, tiled=True),
        lax.all_to_all(send_rows, "lat", split_axis=0, concat_axis=0, tiled=True),
    )
    position = jnp.arange(block_len, dtype=jnp.int32)
    valid_rows = (position[None, None, :] < got_rows[:, :, None]).astype(jnp.float32)
    lat_flat = latents.reshape(cell_count, model_width)
    query_low = jnp.dot(lat_flat, w_query, preferred_element_type=jnp.float32).astype(jnp.bfloat16)
    slot_rows = slot_count * block_len
    step_rows = min(slot_rows, max(block_len, 512))
    step_total = slot_rows // step_rows
    row_items = (
        got_feats.reshape(step_total, step_rows, feat_width),
        got_cells.reshape(step_total, step_rows),
        valid_rows.reshape(step_total, step_rows),
    )

    def forward_step(running_sum, block_item):
        row_feats, row_cell, row_valid = block_item
        term = row_forward(
            query_low, w_key, w_value, row_feats, row_cell, row_valid, head_count, score_scale
        )
        return (running_sum + jax.ops.segment_sum(term, row_cell, num_segments=cell_count), None)

    rows_sum, unused = lax.scan(
        forward_step, jnp.zeros((cell_count, model_width), jnp.float32), row_items
    )
    disk_flat = disk_pixels.reshape(disk_pixels.shape[0], disk_pixels.shape[1], cell_count)
    disk_sum = disk_forward(query_low, disk_flat, w_disk_key, w_disk_value, head_count, score_scale)
    mixed_cells = (rows_sum + disk_sum).astype(jnp.bfloat16)
    updated = (
        lat_flat.astype(jnp.float32)
        + jnp.dot(mixed_cells, w_out, preferred_element_type=jnp.float32)
    ).astype(jnp.bfloat16)
    pred_error = jnp.dot(updated, w_decode, preferred_element_type=jnp.float32) - targets.reshape(
        cell_count, out_width
    )
    row_weight = latitude_weights(tile_lat * lat_count)
    local_weight = lax.dynamic_slice_in_dim(
        row_weight, lax.axis_index("lat") * tile_lat, tile_lat
    ) / jnp.mean(row_weight)
    weight_cell = jnp.repeat(local_weight, tile_lon)
    loss_part = jnp.sum(weight_cell[:, None] * 0.5 * pred_error * pred_error)
    grad_pred = (weight_cell[:, None] * pred_error).astype(jnp.bfloat16)
    grad_upd = jnp.dot(grad_pred, w_decode.T, preferred_element_type=jnp.float32)
    grad_upd_low = grad_upd.astype(jnp.bfloat16)
    grad_mixed = jnp.dot(grad_upd_low, w_out.T, preferred_element_type=jnp.float32)

    def backward_step(carried, block_item):
        grad_query, grad_wkey, grad_wvalue = carried
        row_feats, row_cell, row_valid = block_item
        query_term, step_wkey, step_wvalue, row_grad = row_backward(
            query_low,
            w_key,
            w_value,
            grad_mixed,
            row_feats,
            row_cell,
            row_valid,
            head_count,
            score_scale,
        )
        grad_query = grad_query + jax.ops.segment_sum(query_term, row_cell, num_segments=cell_count)
        return ((grad_query, grad_wkey + step_wkey, grad_wvalue + step_wvalue), row_grad)

    start_state = (
        jnp.zeros((cell_count, model_width), jnp.float32),
        jnp.zeros((feat_width, model_width), jnp.float32),
        jnp.zeros((feat_width, model_width), jnp.float32),
    )
    (query_rows_grad, grad_wkey, grad_wvalue), row_grads = lax.scan(
        backward_step, start_state, row_items
    )
    returned = lax.all_to_all(
        row_grads.reshape(lat_count, capacity, block_len, feat_width),
        "lat",
        split_axis=0,
        concat_axis=0,
        tiled=True,
    )
    row_grad = returned.reshape(slot_count, block_len, feat_width)[slot_of_block].reshape(
        block_count * block_len, feat_width
    )
    query_disk_grad, grad_dkey, grad_dvalue = disk_backward(
        query_low, disk_flat, w_disk_key, w_disk_value, grad_mixed, head_count, score_scale
    )
    grad_query_low = (query_rows_grad + query_disk_grad).astype(jnp.bfloat16)
    latent_grad = grad_upd + jnp.dot(grad_query_low, w_query.T, preferred_element_type=jnp.float32)
    share_rows = model_width // device_count
    loss_scale = 1.0 / (cell_count * device_count * out_width)
    query_full_grad = jnp.dot(lat_flat.T, grad_query_low, preferred_element_type=jnp.float32)
    out_full_grad = jnp.dot(mixed_cells.T, grad_upd_low, preferred_element_type=jnp.float32)
    query_sum, out_sum, key_sum, value_sum, dkey_sum, dvalue_sum, loss_sum = lax.psum(
        (query_full_grad, out_full_grad, grad_wkey, grad_wvalue, grad_dkey, grad_dvalue, loss_part),
        ("lon", "lat"),
    )
    device_index = lax.axis_index(("lon", "lat"))
    update_query = lax.dynamic_slice_in_dim(
        normalized(query_sum), device_index * share_rows, share_rows, 0
    )
    update_out = lax.dynamic_slice_in_dim(
        normalized(out_sum), device_index * share_rows, share_rows, 0
    )
    total_loss = loss_sum * loss_scale
    return (
        total_loss,
        latent_grad.reshape(tile_lat, tile_lon, model_width),
        row_grad,
        update_query,
        update_out,
        normalized(key_sum),
        normalized(value_sum),
        normalized(dkey_sum),
        normalized(dvalue_sum),
    )


def solution(mesh):
    placed = (
        P(("lon", "lat"), None),
        P(("lon", "lat")),
        P(("lon", "lat")),
        P(("lon", "lat")),
        P("lat", "lon", None),
        P(None, None, "lat", "lon"),
        P("lat", "lon", None),
        P(),
        P(),
        P(),
        P(),
        P(),
        P(),
        P(),
    )
    return jax.shard_map(
        body,
        mesh=mesh,
        in_specs=placed,
        out_specs=(
            P(),
            P("lat", "lon", None),
            P(("lon", "lat"), None),
            P(("lon", "lat"), None),
            P(("lon", "lat"), None),
            P(),
            P(),
            P(),
            P(),
        ),
        check_vma=False,
    )
```

profile of v0, /device:TPU:1, one launch (start us, length us, event | category | flops | bytes accessed | tf_op | source)
XLA Modules:
  0.0 1265.4 jit_solution(1457360316976935203)
XLA Ops:
  11.6 8.6 all-to-all-start.2
  28.7 6.7 all-to-all-start
  41.8 4.4 all-to-all-start.1
  46.2 74.0 %while.54 = (s32[]{:T(128)}, f32[512,1024]{0,1:T(8,128)}, bf16[5,16,512]{2,1,0:T(8,128)(2,1)}, bf16[16,1024]{1,0:T(8,128)(2,1)S(1)}, f32[512,1024]{1,0:T(8,128)}...) while((s32[]{:T(128)}, f32[512,1024]{0,1:T(8,128)}, bf16[5,16,512]{2,1,0:T(8,128)(2,1)}, ...), condition=%wide.region_10.11_spmd.clone, body=%wide.region_8.10_spmd.clone.sunk | while | flops 36200448 | bytes 19169392 | solution.py:75
  125.4 199.2 %while.53 = (s32[]{:T(128)}, f32[512,1024]{1,0:T(8,128)}, s32[8,512]{1,0:T(8,128)S(1)}, bf16[512,1024]{1,0:T(8,128)(2,1)S(1)}, bf16[8,512,128]{2,1,0:T(8,128)(2,...) while((s32[]{:T(128)}, f32[512,1024]{1,0:T(8,128)}, ...), condition=%wide.region_7.8_spmd, body=%wide.region_4.7_spmd.sunk | while | flops 271092224 | bytes 26106000 | solution.py:176
  141.8 8.5 scatter_fusion
  166.7 8.5 scatter_fusion
  191.6 8.5 scatter_fusion
  216.5 8.5 scatter_fusion
  241.4 8.5 scatter_fusion
  266.3 8.5 scatter_fusion
  291.2 8.5 scatter_fusion
  316.1 8.5 scatter_fusion
  324.7 13.7 %copy.93 = f32[512,1024]{0,1:T(8,128)} copy(f32[512,1024]{1,0:T(8,128)} %get-tuple-element.197) | data formatting | bytes 4194304 | tf_op jit(solution)/shard_map/while | solution.py:176
  341.9 5.4 fusion.50
  356.5 510.6 %while.55 = (s32[]{:T(128)}, f32[512,1024]{1,0:T(8,128)}, f32[128,1024]{1,0:T(8,128)}, f32[128,1024]{1,0:T(8,128)}, bf16[8,512,128]{2,1,0:T(8,128)(2,1)}, /*inde...) while((s32[]{:T(128)}, f32[512,1024]{1,0:T(8,128)}, ...), condition=%wide.region_17.18_spmd.clone, body=%wide.region_13.17_spmd.clone.sunk | while | flops 814410240 | bytes 87906688 | solution.py:222
  356.5 5.2 gather_fusion.1
  386.5 9.4 scatter_custom_fusion.9
  401.4 4.3 multiply_convert_fusion.16
  420.1 5.2 gather_fusion.1
  450.1 9.4 scatter_custom_fusion.9
  465.0 4.3 multiply_convert_fusion.16
  484.0 5.2 gather_fusion.1
  514.0 9.4 scatter_custom_fusion.9
  528.8 4.3 multiply_convert_fusion.16
  547.8 5.2 gather_fusion.1
  577.8 9.4 scatter_custom_fusion.9
  592.7 4.3 multiply_convert_fusion.16
  611.7 5.2 gather_fusion.1
  641.7 9.4 scatter_custom_fusion.9
  656.6 4.3 multiply_convert_fusion.16
  675.6 5.2 gather_fusion.1
  705.6 9.4 scatter_custom_fusion.9
  739.4 5.2 gather_fusion.1
  769.4 9.4 scatter_custom_fusion.9
  784.3 4.3 multiply_convert_fusion.16
  803.3 5.2 gather_fusion.1
  833.3 9.4 scatter_custom_fusion.9
  848.2 4.3 multiply_convert_fusion.16
  867.1 189.1 %while.56 = (s32[]{:T(128)}, f32[512,1024]{1,0:T(8,128)}, f32[16,1024]{1,0:T(8,128)}, f32[16,1024]{1,0:T(8,128)}, bf16[5,16,512]{2,1,0:T(8,128)(2,1)}, /*index=5...) while((s32[]{:T(128)}, f32[512,1024]{1,0:T(8,128)}, ...), condition=%wide.region_21.22_spmd.clone, body=%wide.region_18.21_spmd.clone.sunk | while | flops 72990720 | bytes 64651544 | solution.py:104
  888.5 4.5 select_add_fusion.2
  925.7 5.2 select_add_fusion.2
  963.6 5.2 select_add_fusion.2
  1001.6 5.2 select_add_fusion.2
  1039.5 5.2 select_add_fusion.2
  1062.2 6.6 all-to-all-start.3
  1068.8 74.8 %psum.49 = f32[]{:T(128)} all-reduce(f32[]{:T(128)} %get-tuple-element.464), channel_id=1, replica_groups=mesh['lon'=8,'lat'=16] {'lon','lat'}, use_global_device_ids=true, to_apply=%region_12.13 | all-reduce | flops 1 | bytes 8 | tf_op jit(solution)/shard_map/psum | solution.py:244
  1151.2 86.0 %all-reduce.3.cloned.1.call-done = (f32[1024,1024]{0,1:T(8,128)}, f32[1024,1024]{1,0:T(8,128)}, f32[128,1024]{1,0:T(8,128)}, f32[128,1024]{1,0:T(8,128)}, f32[16,1024]{1,0:T(8,128)}, /*index=5*/f32[16,1024]{1,0:T(8,128)}) async-done(((f32[1024,1024]{0,1:T(8,128)}, f32[1024,1024]{1,0:T(8,128)}, f32[128,1024]{1,0:T(8,128)}, f32[128,1024]{1,0:T(8,128)}, f32[16,1024]{1,0:T(8,128)}, ...) | async-done | bytes 9568272 | tf_op jit(solution)/shard_map/psum | solution.py:244
  (623 shorter events, 796.3 us)
Async XLA Ops:
  7.2 17.6 %copy-start = (bf16[1024,1024]{1,0:T(8,128)(2,1)S(1)}, bf16[1024,1024]{1,0:T(8,128)(2,1)}, u32[]{:S(2)}) copy-start(bf16[1024,1024]{1,0:T(8,128)(2,1)} %param.29) | copy-start | bytes 6291460
  11.6 17.1 %all-to-all-start.2 = ((s32[16,1,2]{2,1,0:T(1,128)}), s32[16,1,2]{2,1,0:T(1,128)S(1)}, u32[]{:S(2)}, u32[]{:S(2)}) async-start(s32[16,1,2]{2,1,0:T(1,128)} %bitcast.19), calls=%async_computation.2 | async-start | bytes 16384 | tf_op jit(solution)/shard_map/all_to_all | solution.py:154
  28.6 9.2 copy-start.26
  28.7 13.1 %all-to-all-start = ((s32[16,2,128]{2,1,0:T(2,128)}), s32[16,2,128]{2,1,0:T(2,128)S(1)}, u32[]{:S(2)}, u32[]{:S(2)}) async-start(s32[16,2,128]{2,1,0:T(2,128)} %bitcast.15), calls=%async_computation | async-start | bytes 32768 | tf_op jit(solution)/shard_map/all_to_all | solution.py:153
  35.4 10.9 copy-start.8
  35.4 10.9 copy-start.10
  41.8 82.0 %all-to-all-start.1 = ((bf16[16,2,128,128]{3,2,1,0:T(8,128)(2,1)}), bf16[16,2,128,128]{3,2,1,0:T(8,128)(2,1)}, u32[]{:S(2)}, u32[]{:S(2)}) async-start(bf16[16,2,128,128]{3,2,1,0:T(8,128)(2,1)} %broadcast_multiply_fusion), calls=%async_computation.1 | async-start | bytes 2097152 | tf_op jit(solution)/shard_map/all_to_all | solution.py:152
  46.2 1191.0 %all-reduce.3.cloned.1.call-start = ((), (), s32[]{:S(2)}) async-start(), calls=%async_computation.4 | async-start | bytes 19136512 | tf_op jit(solution)/shard_map/psum | solution.py:244
  356.5 510.6 %copy-start.9 = (bf16[16,1024]{1,0:T(8,128)(2,1)S(1)}, bf16[16,1024]{1,0:T(8,128)(2,1)}, u32[]{:S(2)}) copy-start(bf16[16,1024]{1,0:T(8,128)(2,1)} %param.32) | copy-start | bytes 98308
  356.5 510.6 %copy-start.11 = (bf16[16,1024]{1,0:T(8,128)(2,1)S(1)}, bf16[16,1024]{1,0:T(8,128)(2,1)}, u32[]{:S(2)}) copy-start(bf16[16,1024]{1,0:T(8,128)(2,1)} %param.33) | copy-start | bytes 98308
  356.5 5.2 copy-start.24
  356.5 14.2 %copy-start.22 = (f32[8,512]{1,0:T(8,128)}, f32[8,512]{1,0:T(8,128)S(1)}, u32[]{:S(2)}) copy-start(f32[8,512]{1,0:T(8,128)S(1)} %get-tuple-element.806) | copy-start | bytes 49156 | tf_op jit(solution)/shard_map/while
  405.7 5.3 copy-start.2
  405.7 5.3 copy-start.3
  420.1 5.2 copy-start.24
  420.1 14.2 %copy-start.22 = (f32[8,512]{1,0:T(8,128)}, f32[8,512]{1,0:T(8,128)S(1)}, u32[]{:S(2)}) copy-start(f32[8,512]{1,0:T(8,128)S(1)} %get-tuple-element.806) | copy-start | bytes 49156 | tf_op jit(solution)/shard_map/while
  469.3 5.6 copy-start.2
  469.3 5.6 copy-start.3
  483.9 5.2 copy-start.24
  483.9 14.2 %copy-start.22 = (f32[8,512]{1,0:T(8,128)}, f32[8,512]{1,0:T(8,128)S(1)}, u32[]{:S(2)}) copy-start(f32[8,512]{1,0:T(8,128)S(1)} %get-tuple-element.806) | copy-start | bytes 49156 | tf_op jit(solution)/shard_map/while
  533.1 5.6 copy-start.2
  533.1 5.6 copy-start.3
  547.8 5.2 copy-start.24
  547.8 14.2 %copy-start.22 = (f32[8,512]{1,0:T(8,128)}, f32[8,512]{1,0:T(8,128)S(1)}, u32[]{:S(2)}) copy-start(f32[8,512]{1,0:T(8,128)S(1)} %get-tuple-element.806) | copy-start | bytes 49156 | tf_op jit(solution)/shard_map/while
  597.0 5.6 copy-start.2
  597.0 5.6 copy-start.3
  611.6 5.2 copy-start.24
  611.6 14.2 %copy-start.22 = (f32[8,512]{1,0:T(8,128)}, f32[8,512]{1,0:T(8,128)S(1)}, u32[]{:S(2)}) copy-start(f32[8,512]{1,0:T(8,128)S(1)} %get-tuple-element.806) | copy-start | bytes 49156 | tf_op jit(solution)/shard_map/while
  660.9 5.6 copy-start.2
  660.9 5.6 copy-start.3
  675.5 5.2 copy-start.24
  675.5 14.2 %copy-start.22 = (f32[8,512]{1,0:T(8,128)}, f32[8,512]{1,0:T(8,128)S(1)}, u32[]{:S(2)}) copy-start(f32[8,512]{1,0:T(8,128)S(1)} %get-tuple-element.806) | copy-start | bytes 49156 | tf_op jit(solution)/shard_map/while
  724.7 5.6 copy-start.2
  724.7 5.6 copy-start.3
  739.4 5.2 copy-start.24
  739.4 14.2 %copy-start.22 = (f32[8,512]{1,0:T(8,128)}, f32[8,512]{1,0:T(8,128)S(1)}, u32[]{:S(2)}) copy-start(f32[8,512]{1,0:T(8,128)S(1)} %get-tuple-element.806) | copy-start | bytes 49156 | tf_op jit(solution)/shard_map/while
  788.6 5.6 copy-start.2
  788.6 5.6 copy-start.3
  803.2 5.2 copy-start.24
  803.2 14.2 %copy-start.22 = (f32[8,512]{1,0:T(8,128)}, f32[8,512]{1,0:T(8,128)S(1)}, u32[]{:S(2)}) copy-start(f32[8,512]{1,0:T(8,128)S(1)} %get-tuple-element.806) | copy-start | bytes 49156 | tf_op jit(solution)/shard_map/while
  852.4 5.6 copy-start.2
  852.4 5.6 copy-start.3
  1062.2 6.6 copy-start.27
  1062.2 86.3 %all-to-all-start.3 = ((bf16[16,2,128,128]{3,2,1,0:T(8,128)(2,1)}), bf16[16,2,128,128]{3,2,1,0:T(8,128)(2,1)}, u32[]{:S(2)}, u32[]{:S(2)}) async-start(bf16[16,2,128,128]{3,2,1,0:T(8,128)(2,1)} %bitcast.254), calls=%async_computation.3 | async-start | bytes 2097152 | tf_op jit(solution)/shard_map/all_to_all | solution.py:225
  1243.8 6.1 copy-start.17
  1243.8 6.1 copy-start.18
  1247.7 6.0 copy-start.20
  1247.8 6.0 copy-start.21
  (62 other events, 155.3 us)
Sparse Core Ops, SparseCore 0:
  1062.3 174.8 all-reduce.2
where the time goes:
time: 1280 us; the launch traced here: 1270 us
  local copies, waits for them, and re-layouts  425 us (33%)
  other arithmetic  344 us (27%)
  matrix products  283 us (22%)
  waiting for transfers between devices  89.4 us (7%)
  blocking collectives  74.8 us (6%)
  starting transfers between devices  26.3 us (2%)
  between operations  21.3 us (2%)
    mul x42, local copies, waits for them, and re-layouts, per_head(): head_weights[:, :, None] * values.reshape(values.shape[0], head_count, -1)  94.6 us
    psum x1, waiting for transfers between devices, body(): lax.psum((query_full_grad, out_full_grad, grad_wkey, grad_wvalue, grad_dk...  86 us
    reduce_sum x39, other arithmetic, head_sums(): return jnp.sum(product.reshape(product.shape[0], head_count, -1), axis=2)  79.3 us
    scatter-add x8, other arithmetic, backward_step(): jax.ops.segment_sum(query_term, row_cell, num_segments=cell_count)  75.4 us
    psum x1, blocking collectives, body(): lax.psum((query_full_grad, out_full_grad, grad_wkey, grad_wvalue, grad_dk...  74.8 us
    scatter-add x8, other arithmetic, forward_step(): jax.ops.segment_sum(term, row_cell, num_segments=cell_count)  68.4 us
    gather x16, local copies, waits for them, and re-layouts, row_backward(): grad_rows = grad_mixed[row_cell]  64.8 us
    dot_general x10, matrix products, one_disk(): disk_key = jnp.dot(pixels.T, w_disk_key, preferred_element_type=jnp.float32)  37.6 us
  transfers between devices with their start and end apart: 5, of which 2 were waited for; matrix products, arithmetic and copies ran while one was open for 8% of the time, Pallas kernels for 0%

commit v1 on v0

v1 whole, which is shorter than its diff:
```python
import functools
import math

import jax
import jax.numpy as jnp
import numpy as np
from jax import lax
from jax.experimental import pallas as pl
from jax.experimental.pallas import tpu as pltpu
from jax.sharding import PartitionSpec as P

HEADS = 16
CAP = 2
CHUNK = 256
F32 = jnp.float32
BF16 = jnp.bfloat16

NN = (((1,), (0,)), ((), ()))
NT = (((1,), (1,)), ((), ()))
TN = (((0,), (0,)), ((), ()))


def mm(a, b, dims=NN):
    return lax.dot_general(a, b, dims, preferred_element_type=F32)


def vmem():
    return pl.BlockSpec(memory_space=pltpu.VMEM)


def smem():
    return pl.BlockSpec(memory_space=pltpu.SMEM)


def pack_kernel(tile_ref, rows_ref, feats_ref, cells_ref, sfeats_ref, scells_ref, slot_ref, count):
    block_count, block_len = cells_ref.shape
    tile_total = sfeats_ref.shape[0] // (CAP * block_len)
    scells_ref[...] = jnp.full(scells_ref.shape, -1, jnp.int32)
    for t in range(tile_total):
        count[t] = 0
    lane = lax.broadcasted_iota(jnp.int32, (1, block_len), 1)
    for b in range(block_count):
        t = tile_ref[b]
        n = count[t]
        count[t] = n + 1
        slot = t * CAP + n
        slot_ref[b] = slot
        sfeats_ref[pl.ds(pl.multiple_of(slot * block_len, block_len), block_len), :] = feats_ref[
            b * block_len : (b + 1) * block_len, :
        ]
        scells_ref[pl.ds(slot, 1), :] = jnp.where(lane < rows_ref[b], cells_ref[b : b + 1, :], -1)


def pack(block_tile, block_rows, radiances, row_cells, lat_count):
    block_count = block_tile.shape[0]
    rows, feat = radiances.shape
    block_len = rows // block_count
    slots = lat_count * CAP
    return pl.pallas_call(
        pack_kernel,
        out_shape=(
            jax.ShapeDtypeStruct((slots * block_len, feat), BF16),
            jax.ShapeDtypeStruct((slots, block_len), jnp.int32),
            jax.ShapeDtypeStruct((block_count,), jnp.int32),
        ),
        in_specs=[smem(), smem(), vmem(), vmem()],
        out_specs=(vmem(), vmem(), smem()),
        scratch_shapes=[pltpu.SMEM((lat_count,), jnp.int32)],
        name="pack",
    )(block_tile, block_rows, radiances, row_cells.reshape(block_count, block_len))


def tile_kernel(
    weight_ref,
    feats_ref,
    cells_ref,
    lat_ref,
    disk_ref,
    target_ref,
    wq_ref,
    wkv_ref,
    wdk_ref,
    wdv_ref,
    wo_ref,
    wd_ref,
    lgrad_ref,
    rgrad_ref,
    gq_ref,
    go_ref,
    gs_ref,
    loss_ref,
    comp,
    cellb,
    kv,
    qr,
    gate,
    acc,
    gkv,
    query,
    mixed,
    gul,
    gmix,
    px,
    bkt,
    bvt,
    gdisk,
    mdisk,
    hsum,
    hspread,
    countv,
    counts,
    csem,
    osem,
):
    slots, block_len = cells_ref.shape
    cells, width = lat_ref.shape
    feat = feats_ref.shape[1]
    disks_ch = disk_ref.shape[0]
    ch = wdk_ref.shape[0]
    disks = disks_ch // ch
    hd = width // HEADS
    scale = 1.0 / math.sqrt(hd)
    out_width = target_ref.shape[1]
    hl = hsum.shape[1]
    cw = ch * HEADS
    grid_rows = cells // 128

    valid = (cells_ref[...] >= 0).astype(jnp.int32)
    countv[...] = jnp.broadcast_to(jnp.sum(valid, axis=1, keepdims=True), countv.shape)
    copy = pltpu.make_async_copy(countv, counts, csem)
    copy.start()

    hsum[...] = jnp.where(
        lax.broadcasted_iota(jnp.int32, (width, hl), 0) // hd
        == lax.broadcasted_iota(jnp.int32, (width, hl), 1),
        1.0,
        0.0,
    ).astype(BF16)
    hspread[...] = jnp.where(
        lax.broadcasted_iota(jnp.int32, (hl, width), 1) // hd
        == lax.broadcasted_iota(jnp.int32, (hl, width), 0),
        1.0,
        0.0,
    ).astype(BF16)
    comp[...] = jnp.zeros(comp.shape, BF16)
    cellb[...] = jnp.full(cellb.shape, -1, jnp.int32)

    def project(i, _):
        r = pl.ds(pl.multiple_of(i * CHUNK, CHUNK), CHUNK)
        query[r, :] = mm(lat_ref[r, :], wq_ref[...]).astype(BF16)
        return 0

    lax.fori_loop(0, cells // CHUNK, project, 0)

    spread_ch = jnp.where(
        lax.broadcasted_iota(jnp.int32, (cw, ch), 0) // HEADS
        == lax.broadcasted_iota(jnp.int32, (cw, ch), 1),
        1.0,
        0.0,
    ).astype(BF16)
    head_mask = (
        lax.broadcasted_iota(jnp.int32, (cw, width), 0) % HEADS
        == lax.broadcasted_iota(jnp.int32, (cw, width), 1) // hd
    )
    bkt[...] = jnp.where(head_mask, mm(spread_ch, wdk_ref[...]), 0.0).astype(BF16)
    bvt[...] = jnp.where(head_mask, mm(spread_ch, wdv_ref[...]), 0.0).astype(BF16)
    sum_ch = jnp.where(
        lax.broadcasted_iota(jnp.int32, (cw, hl), 0) % HEADS
        == lax.broadcasted_iota(jnp.int32, (cw, hl), 1),
        1.0,
        0.0,
    ).astype(BF16)
    qt = mm(query[...], bkt[...], NT)
    msum = jnp.zeros((cells, cw), F32)
    for k in range(disks):
        pxk = mm(
            disk_ref[k * ch : (k + 1) * ch, :], spread_ch, (((0,), (1,)), ((), ()))
        )
        px[:, k * cw : (k + 1) * cw] = pxk.astype(BF16)
        g = jax.nn.sigmoid(mm((pxk * qt).astype(BF16), sum_ch) * scale)
        gdisk[:, k * hl : (k + 1) * hl] = g
        msum = msum + mm(g.astype(BF16), sum_ch, NT) * pxk
    mdisk[...] = msum.astype(BF16)

    def disk_mix(i, _):
        r = pl.ds(pl.multiple_of(i * CHUNK, CHUNK), CHUNK)
        acc[r, :] = mm(mdisk[r, :], bvt[...])
        return 0

    lax.fori_loop(0, cells // CHUNK, disk_mix, 0)

    copy.wait()
    padded = jnp.concatenate(
        [cells_ref[...], jnp.full((block_len - slots, block_len), -1, jnp.int32)], axis=0
    )
    columns = jnp.transpose(padded.astype(F32)).astype(jnp.int32)
    row = lax.broadcasted_iota(jnp.int32, (block_len, feat), 0)
    offset = jnp.int32(0)
    for s in range(slots):
        at = pl.ds(pl.multiple_of(offset, 16), block_len)
        got = feats_ref[s * block_len : (s + 1) * block_len, :]
        comp[at, :] = jnp.where(row < counts[s, 0], got, jnp.zeros_like(got))
        cellb[at, :] = jnp.broadcast_to(columns[:, s : s + 1], (block_len, 128))
        offset = offset + ((counts[s, 0] + 15) // 16) * 16
    chunk_total = (offset + (CHUNK - 1)) // CHUNK

    lane = lax.broadcasted_iota(jnp.int32, (CHUNK, 128), 1)

    def one_hot(r):
        cb = cellb[r, :]
        return jnp.concatenate(
            [
                jnp.where(cb == lane + 128 * j, 1.0, 0.0).astype(BF16)
                for j in range(cells // 128)
            ],
            axis=1,
        )

    def forward(i, _):
        r = pl.ds(pl.multiple_of(i * CHUNK, CHUNK), CHUNK)
        f = comp[r, :]
        both = mm(f, wkv_ref[...])
        low = both.astype(BF16)
        kv[r, :] = low
        oh = one_hot(r)
        q = mm(oh, query[...]).astype(BF16)
        qr[r, :] = q
        g = jax.nn.sigmoid(mm(q * low[:, :width], hsum[...]) * scale)
        gate[r, :] = g
        term = mm(g.astype(BF16), hspread[...]).astype(BF16) * low[:, width:]
        acc[...] += mm(oh, term, TN)
        return 0

    lax.fori_loop(0, chunk_total, forward, 0)

    lat_at = lax.axis_index("lat") * grid_rows
    tile = 128

    def middle(i, loss):
        r = pl.ds(pl.multiple_of(i * tile, tile), tile)
        m = acc[r, :].astype(BF16)
        mixed[r, :] = m
        updated = (lat_ref[r, :].astype(F32) + mm(m, wo_ref[...])).astype(BF16)
        err = mm(updated, wd_ref[...]) - target_ref[r, :]
        w = weight_ref[lat_at + i]
        gp = w * err
        gu = mm(gp.astype(BF16), wd_ref[...], NT)
        lgrad_ref[r, :] = gu
        gu_low = gu.astype(BF16)
        gul[r, :] = gu_low
        gmix[r, :] = mm(gu_low, wo_ref[...], NT).astype(BF16)
        return loss + jnp.sum((0.5 * gp * err).reshape(tile // 8, 8, out_width), axis=0)

    loss_ref[...] = lax.fori_loop(0, cells // tile, middle, jnp.zeros((8, out_width), F32))

    gt = mm(gmix[...], bvt[...], NT)
    nsum = jnp.zeros((cells, cw), F32)
    for k in range(disks):
        pxk = px[:, k * cw : (k + 1) * cw].astype(F32)
        g = gdisk[:, k * hl : (k + 1) * hl]
        ds = mm((pxk * gt).astype(BF16), sum_ch) * g * (1.0 - g) * scale
        nsum = nsum + mm(ds.astype(BF16), sum_ch, NT) * pxk
    ndisk = nsum.astype(BF16)

    def disk_weight(left, right):
        full = jnp.where(head_mask, mm(left, right, TN), 0.0)
        return jnp.sum(full.reshape(ch, HEADS, width), axis=1)

    gs_ref[2 * feat : 2 * feat + ch, :] = disk_weight(ndisk, query[...]).astype(gs_ref.dtype)
    gs_ref[2 * feat + ch :, :] = disk_weight(mdisk[...], gmix[...]).astype(gs_ref.dtype)
    mdisk[...] = ndisk

    def disk_query(i, _):
        r = pl.ds(pl.multiple_of(i * CHUNK, CHUNK), CHUNK)
        acc[r, :] = mm(mdisk[r, :], bkt[...])
        return 0

    lax.fori_loop(0, cells // CHUNK, disk_query, 0)
    gkv[...] = jnp.zeros(gkv.shape, F32)

    def backward(i, _):
        r = pl.ds(pl.multiple_of(i * CHUNK, CHUNK), CHUNK)
        oh = one_hot(r)
        gm = mm(oh, gmix[...]).astype(BF16)
        g = gate[r, :]
        ds = mm(gm * kv[r, width:], hsum[...]) * g * (1.0 - g) * scale
        ds_wide = mm(ds.astype(BF16), hspread[...]).astype(BF16)
        acc[...] += mm(oh, ds_wide * kv[r, :width], TN)
        g_wide = mm(g.astype(BF16), hspread[...]).astype(BF16)
        grads = jnp.concatenate([ds_wide * qr[r, :], g_wide * gm], axis=1)
        gkv[...] += mm(comp[r, :], grads, TN)
        comp[r, :] = mm(grads, wkv_ref[...], NT).astype(BF16)
        return 0

    lax.fori_loop(0, chunk_total, backward, 0)
    gs_ref[:feat, :] = gkv[:, :width].astype(gs_ref.dtype)
    gs_ref[feat : 2 * feat, :] = gkv[:, width:].astype(gs_ref.dtype)

    offset = jnp.int32(0)
    for s in range(slots):
        at = pl.ds(pl.multiple_of(offset, 16), block_len)
        got = comp[at, :]
        rgrad_ref[s * block_len : (s + 1) * block_len, :] = jnp.where(
            row < counts[s, 0], got, jnp.zeros_like(got)
        )
        offset = offset + ((counts[s, 0] + 15) // 16) * 16

    def finish(i, _):
        r = pl.ds(pl.multiple_of(i * tile, tile), tile)
        gq = acc[r, :].astype(BF16)
        query[r, :] = gq
        lgrad_ref[r, :] += mm(gq, wq_ref[...], NT)
        return 0

    lax.fori_loop(0, cells // tile, finish, 0)

    def weights(i, _):
        at = pl.multiple_of(i * CHUNK, CHUNK)
        c = pl.ds(at, CHUNK)
        later = pl.ds(pl.multiple_of(width + i * CHUNK, CHUNK), CHUNK)
        qr[c, :] = mm(lat_ref[:, c], query[...], TN).astype(BF16)
        pltpu.make_async_copy(qr.at[c], gq_ref.at[c], osem.at[0, i]).start()
        qr[later, :] = mm(mixed[:, c], gul[...], TN).astype(BF16)
        pltpu.make_async_copy(qr.at[later], go_ref.at[c], osem.at[1, i]).start()
        return 0

    lax.fori_loop(0, width // CHUNK, weights, 0)
    for i in range(width // CHUNK):
        c = slice(i * CHUNK, (i + 1) * CHUNK)
        later = slice(width + i * CHUNK, width + (i + 1) * CHUNK)
        pltpu.make_async_copy(qr.at[c], gq_ref.at[c], osem.at[0, i]).wait()
        pltpu.make_async_copy(qr.at[later], go_ref.at[c], osem.at[1, i]).wait()


def tile_step(weight, feats, cells, lat_flat, disk, target, wq, wkv, wdk, wdv, wo, wd):
    rows, feat = feats.shape
    cell_count, width = lat_flat.shape
    ch = wdk.shape[0]
    disks = disk.shape[0] // ch
    cw = ch * HEADS
    slots = cells.shape[0]
    return pl.pallas_call(
        tile_kernel,
        out_shape=(
            jax.ShapeDtypeStruct((cell_count, width), F32),
            jax.ShapeDtypeStruct((rows, feat), BF16),
            jax.ShapeDtypeStruct((width, width), BF16),
            jax.ShapeDtypeStruct((width, width), BF16),
            jax.ShapeDtypeStruct((2 * feat + 2 * ch, width), BF16),
            jax.ShapeDtypeStruct((8, target.shape[1]), F32),
        ),
        in_specs=[smem()] + [vmem()] * 11,
        out_specs=(vmem(), vmem(), pl.BlockSpec(memory_space=pl.ANY), pl.BlockSpec(memory_space=pl.ANY), vmem(), vmem()),
        scratch_shapes=[
            pltpu.VMEM((rows, feat), BF16),
            pltpu.VMEM((rows, 128), jnp.int32),
            pltpu.VMEM((rows, 2 * width), BF16),
            pltpu.VMEM((rows, width), BF16),
            pltpu.VMEM((rows, 128), F32),
            pltpu.VMEM((cell_count, width), F32),
            pltpu.VMEM((feat, 2 * width), F32),
            pltpu.VMEM((cell_count, width), BF16),
            pltpu.VMEM((cell_count, width), BF16),
            pltpu.VMEM((cell_count, width), BF16),
            pltpu.VMEM((cell_count, width), BF16),
            pltpu.VMEM((cell_count, disks * cw), BF16),
            pltpu.VMEM((cw, width), BF16),
            pltpu.VMEM((cw, width), BF16),
            pltpu.VMEM((cell_count, disks * 128), F32),
            pltpu.VMEM((cell_count, cw), BF16),
            pltpu.VMEM((width, 128), BF16),
            pltpu.VMEM((128, width), BF16),
            pltpu.VMEM((slots, 128), jnp.int32),
            pltpu.SMEM((slots, 128), jnp.int32),
            pltpu.SemaphoreType.DMA,
            pltpu.SemaphoreType.DMA((2, width // CHUNK)),
        ],
        compiler_params=pltpu.CompilerParams(vmem_limit_bytes=62 * 1024 * 1024),
        name="tile",
    )(weight, feats, cells, lat_flat, disk, target, wq, wkv, wdk, wdv, wo, wd)


def unpack_kernel(slot_ref, got_ref, out_ref):
    block_count = slot_ref.shape[0]
    block_len = out_ref.shape[0] // block_count
    for b in range(block_count):
        out_ref[b * block_len : (b + 1) * block_len, :] = got_ref[
            pl.ds(pl.multiple_of(slot_ref[b] * block_len, block_len), block_len), :
        ]


def unpack(slots, got, rows):
    return pl.pallas_call(
        unpack_kernel,
        out_shape=jax.ShapeDtypeStruct((rows, got.shape[1]), BF16),
        in_specs=[smem(), vmem()],
        out_specs=vmem(),
        name="unpack",
    )(slots, got)


def cell_weights(row_total):
    centres = (np.arange(row_total, dtype=np.float32) + np.float32(0.5)) / np.float32(row_total)
    weight = np.cos(np.float32(math.pi / 180.0) * (np.float32(-60.0) + np.float32(120.0) * centres))
    return (weight / np.mean(weight)).astype(np.float32)


def body(
    radiances,
    block_tile,
    block_rows,
    row_cells,
    latents,
    disk_pixels,
    targets,
    w_query,
    w_key,
    w_value,
    w_disk_key,
    w_disk_value,
    w_out,
    w_decode,
):
    lat_count = lax.axis_size("lat")
    device_count = lax.axis_size(("lon", "lat"))
    rows = radiances.shape[0]
    tile_lat, tile_lon, width = latents.shape
    out_width = targets.shape[2]
    cells = tile_lat * tile_lon
    feat = radiances.shape[1]
    ch = w_disk_key.shape[0]
    sfeats, scells, slot = pack(block_tile, block_rows, radiances, row_cells, lat_count)
    got_feats = lax.all_to_all(
        sfeats.reshape(lat_count, -1, feat), "lat", split_axis=0, concat_axis=0, tiled=True
    ).reshape(sfeats.shape)
    got_cells = lax.all_to_all(
        scells.reshape(lat_count, CAP, -1), "lat", split_axis=0, concat_axis=0, tiled=True
    ).reshape(scells.shape)
    weight = jnp.asarray(cell_weights(tile_lat * lat_count))
    lgrad, rgrad, gq, go, gs, loss = tile_step(
        weight,
        got_feats,
        got_cells,
        latents.reshape(cells, width),
        disk_pixels.reshape(-1, cells),
        targets.reshape(cells, out_width),
        w_query,
        jnp.concatenate([w_key, w_value], axis=1),
        w_disk_key,
        w_disk_value,
        w_out,
        w_decode,
    )
    returned = lax.all_to_all(
        rgrad.reshape(lat_count, -1, feat), "lat", split_axis=0, concat_axis=0, tiled=True
    ).reshape(rgrad.shape)
    row_grad = unpack(slot, returned, rows)
    axes = ("lon", "lat")
    gq_share = lax.psum_scatter(gq.astype(F32), axes, scatter_dimension=0, tiled=True)
    go_share = lax.psum_scatter(go.astype(F32), axes, scatter_dimension=0, tiled=True)
    gs_sum, loss_sum, sq, so = lax.psum(
        (
            gs.astype(F32),
            jnp.sum(loss),
            jnp.sum(gq_share * gq_share),
            jnp.sum(go_share * go_share),
        ),
        axes,
    )
    entries = width * width
    small = []
    at = 0
    for n in (feat, feat, ch, ch):
        g = gs_sum[at : at + n]
        small.append(g / jnp.sqrt(jnp.mean(g * g) + 1e-06))
        at += n
    return (
        loss_sum * (1.0 / (cells * device_count * out_width)),
        lgrad.reshape(latents.shape),
        row_grad,
        gq_share / jnp.sqrt(sq / entries + 1e-06),
        go_share / jnp.sqrt(so / entries + 1e-06),
        *small,
    )


def solution(mesh):
    both = ("lon", "lat")
    placed = (
        P(both, None),
        P(both),
        P(both),
        P(both),
        P("lat", "lon", None),
        P(None, None, "lat", "lon"),
        P("lat", "lon", None),
    ) + (P(),) * 7
    return jax.shard_map(
        body,
        mesh=mesh,
        in_specs=placed,
        out_specs=(
            P(),
            P("lat", "lon", None),
            P(both, None),
            P(both, None),
            P(both, None),
            P(),
            P(),
            P(),
            P(),
        ),
        check_vma=False,
    )
```

time: 1280 us -> 1490 us (1.16)
  waiting for transfers between devices: 89.4 us -> 1260 us
  local copies, waits for them, and re-layouts: 425 us -> 4.18 us
  other arithmetic: 344 us -> 14.3 us
  matrix products: 283 us -> 0 us
  Pallas kernels: 0 us -> 47.2 us
  blocking collectives: 74.8 us -> 115 us
    reduce_scatter x0 -> x2, waiting for transfers between devices: none -> 1250 us  [the longest x1 640 us: body(): lax.psum_scatter(go.astype(F32), axes, scatter_dimension=0, tiled=True)]
    dot_general x101 -> x0, matrix products: 283 us -> none  [the longest x10 37.6 us: one_disk(): disk_key = jnp.dot(pixels.T, w_disk_key, preferred_element_type=jnp.float32)]
    mul x82 -> x0, local copies, waits for them, and re-layouts: 209 us -> none  [the longest x42 94.6 us: per_head(): head_weights[:, :, None] * values.reshape(values.shape[0], head_count, -1)]
    scatter-add x16 -> x0, other arithmetic: 144 us -> none  [the longest x8 75.4 us: backward_step(): jax.ops.segment_sum(query_term, row_cell, num_segments=cell_count)]
    gather x36 -> x0, local copies, waits for them, and re-layouts: 118 us -> none  [the longest x16 64.8 us: row_backward(): grad_rows = grad_mixed[row_cell]]
    psum x1 -> x0, waiting for transfers between devices: 86 us -> none  [body(): lax.psum((query_full_grad, out_full_grad, grad_wkey, grad_wvalue, grad_dk...]
    reduce_sum x46 -> x5, other arithmetic: 90.2 us -> 4.7 us  [the longest x1 1.37 us: body(): jnp.sum(gq_share * gq_share)]
    while x190 -> x0, local copies, waits for them, and re-layouts: 48.9 us -> none
  transfers between devices with their start and end apart: 5 -> 4, of which waited for: 2 -> 3; matrix products, arithmetic and copies ran while one was open for 8% -> 0% of each run, Pallas kernels for 0% -> 0%
where the time goes in v1:
time: 1490 us; the launch traced here: 1480 us
  waiting for transfers between devices  1260 us (85%)
  blocking collectives  115 us (8%)
  Pallas kernels  47.2 us (3%)
  starting transfers between devices  21.6 us (1%)
  between operations  20.1 us (1%)
    reduce_scatter x1, waiting for transfers between devices, body(): lax.psum_scatter(go.astype(F32), axes, scatter_dimension=0, tiled=True)  640 us
    reduce_scatter x1, waiting for transfers between devices, body(): lax.psum_scatter(gq.astype(F32), axes, scatter_dimension=0, tiled=True)  609 us
    psum x1, blocking collectives, body(): lax.psum((gs.astype(F32), jnp.sum(loss), jnp.sum(gq_share * gq_share), jn...  99.8 us
    pallas_call x1, Pallas kernels, tile_step(): pl.pallas_call(tile_kernel, out_shape=(jax.ShapeDtypeStruct((cell_count,...  43 us
  transfers between devices with their start and end apart: 4, of which 3 were waited for; matrix products, arithmetic and copies ran while one was open for 0% of the time, Pallas kernels for 0%

profile of v1, /device:TPU:1, one launch (start us, length us, event | category | flops | bytes accessed | tf_op | source)
XLA Modules:
  0.0 1484.7 jit_solution(14826080087361343762)
XLA Ops:
  7.2 0.0 copy-start.8
  7.2 0.0 copy-start.4
  7.2 0.0 copy-start.5
  7.2 2.2 pack.1
  9.4 15.2 %all_to_all.15 = s32[16,2,128]{2,1,0:T(2,128)} all-to-all(s32[16,2,128]{2,1,0:T(2,128)} %bitcast.23), channel_id=1, replica_groups=mesh['lon'=8,'lat'=16] {'lat'}, dimensions={0} | all-to-all | bytes 32768 | tf_op jit(solution)/shard_map/all_to_all | solution.py:436
  24.6 3.7 all-to-all-start
  28.2 0.0 reduce-scatter.3.cloned.1.call-start
  28.3 0.0 copy-done.8
  28.3 0.6 copy.26
  28.9 0.0 copy-done.4
  28.9 0.0 copy-done.5
  28.9 0.8 pad_maximum_fusion.wkv_ref
  29.8 13.3 all-to-all-done
  43.0 0.0 copy-start.1
  43.0 1.0 copy-done.1
  44.0 43.0 %tile.1 = (f32[512,1024]{1,0:T(8,128)}, bf16[4096,128]{1,0:T(8,128)(2,1)}, bf16[1024,1024]{1,0:T(8,128)(2,1)}, bf16[1024,1024]{1,0:T(8,128)(2,1)}, bf16[288,1024]{1,0:T(8,128)(2,1)}, /*index=5*/f32[8,128]{1,0:T(8,128)}) custom-call(f32[64]{0:T(128)} %constant.20.clone.weight_ref, bf16[4096,128]{1,0:T(8,128)(2,1)} %bitcast.16, s32[32,128]{1,0:T(8,128)} %bitcast.22, ...), custom_call_target="tpu_custom_call" | custom-call | tf_op jit(solution)/shard_map/tile/pallas_call | solution.py:342
  87.0 4.0 convert_element_type.9
  91.0 0.0 copy-start.2
  91.0 0.0 reduce-scatter.3.cloned.1.call-update
  91.0 0.0 reduce-scatter.5.cloned.1.call-start
  91.1 1.5 copy-done.2
  92.6 2.4 convert_element_type.10
  95.0 0.0 reduce-scatter.5.cloned.1.call-update
  95.0 0.0 copy-start.9
  95.0 0.0 copy-start.3
  95.1 17.9 %all-to-all-start.2 = ((bf16[16,256,128]{2,1,0:T(8,128)(2,1)}), bf16[16,256,128]{2,1,0:T(8,128)(2,1)S(1)}, u32[]{:S(2)}, u32[]{:S(2)}) async-start(bf16[16,256,128]{2,1,0:T(8,128)(2,1)} %bitcast.8), calls=%async_computation.2 | async-start | bytes 2097152 | tf_op jit(solution)/shard_map/all_to_all | solution.py:454
  113.0 0.0 copy-done.9
  113.0 0.6 reduce_sum.63
  113.6 609.0 %reduce-scatter.3.cloned.1.call-done = f32[8,1024]{1,0:T(8,128)} async-done(((f32[1024,1024]{1,0:T(8,128)}), f32[8,1024]{1,0:T(8,128)}) %reduce-scatter.3.cloned.1.call-update) | async-done | bytes 32784 | tf_op jit(solution)/shard_map/reduce_scatter | solution.py:459
  722.6 1.4 multiply_reduce_fusion.5
  724.0 639.9 %reduce-scatter.5.cloned.1.call-done = f32[8,1024]{1,0:T(8,128)} async-done(((f32[1024,1024]{1,0:T(8,128)}), f32[8,1024]{1,0:T(8,128)}) %reduce-scatter.5.cloned.1.call-update) | async-done | bytes 32784 | tf_op jit(solution)/shard_map/reduce_scatter | solution.py:460
  1363.9 1.4 multiply_reduce_fusion.4
  1365.3 0.0 all-to-all-done.2
  1365.3 0.0 copy-start
  1365.3 1.0 copy-done
  1366.3 2.1 unpack.1
  1368.3 0.0 copy-done.3
  1368.3 0.0 copy-start.6
  1368.4 0.0 copy-start.7
  1368.4 99.8 %all-reduce.2 = (f32[]{:T(128)}, f32[]{:T(128)}, f32[]{:T(128)}, f32[288,1024]{1,0:T(8,128)S(1)}) all-reduce(f32[]{:T(128)} %reduce_sum.63, f32[]{:T(128)} %multiply_reduce_fusion.5, f32[]{:T(128)} %multiply_reduce_fusion.4, bf16[288,1024]{1,0:T(8,128)(2,1)S(1)} %copy-done.3), channel_id=1, replica_groups=mesh['lon'=8,'lat'=16] {'lon','lat'}, use_global_device_ids=true, to_apply=%region_1.0 | all-reduce | flops 294915 | bytes 1769496 | tf_op jit(solution)/shard_map/psum | solution.py:461
  1468.2 0.7 multiply_reduce_fusion
  1468.9 0.6 multiply_reduce_fusion.2
  1474.3 1.1 slice_divide_fusion
  1475.4 0.7 slice_divide_fusion.2
  1476.1 0.0 copy-done.6
  1476.1 0.0 copy-done.7
  1476.1 0.6 broadcast_divide_fusion
Async XLA Ops:
  7.2 21.1 %copy-start.8 = (bf16[5,16,4,128]{3,2,1,0:T(4,128)(2,1)S(1)}, bf16[5,16,4,128]{3,2,1,0:T(4,128)(2,1)}, u32[]{:S(2)}) copy-start(bf16[5,16,4,128]{3,2,1,0:T(4,128)(2,1)} %param.20) | copy-start | bytes 245764
  7.2 21.7 %copy-start.4 = (bf16[128,1024]{1,0:T(8,128)(2,1)S(1)}, bf16[128,1024]{1,0:T(8,128)(2,1)}, u32[]{:S(2)}) copy-start(bf16[128,1024]{1,0:T(8,128)(2,1)} %param.24) | copy-start | bytes 786436
  7.2 21.7 %copy-start.5 = (bf16[128,1024]{1,0:T(8,128)(2,1)S(1)}, bf16[128,1024]{1,0:T(8,128)(2,1)}, u32[]{:S(2)}) copy-start(bf16[128,1024]{1,0:T(8,128)(2,1)} %param.23) | copy-start | bytes 786436
  24.6 18.5 %all-to-all-start = ((bf16[16,256,128]{2,1,0:T(8,128)(2,1)}), bf16[16,256,128]{2,1,0:T(8,128)(2,1)S(1)}, u32[]{:S(2)}, u32[]{:S(2)}) async-start(bf16[16,256,128]{2,1,0:T(8,128)(2,1)} %bitcast.17), calls=%async_computation | async-start | bytes 2097152 | tf_op jit(solution)/shard_map/all_to_all | solution.py:433
  28.2 694.4 %reduce-scatter.3.cloned.1.call-start = ((), (), s32[]{:S(2)}) async-start(), calls=%async_computation.5 | async-start | bytes 4227072 | tf_op jit(solution)/shard_map/reduce_scatter | solution.py:459
  43.0 1.0 copy-start.1
  91.0 1.6 copy-start.2
  91.0 1272.9 %reduce-scatter.5.cloned.1.call-start = ((), (), s32[]{:S(2)}) async-start(), calls=%async_computation.6 | async-start | bytes 4227072 | tf_op jit(solution)/shard_map/reduce_scatter | solution.py:460
  95.0 17.9 %copy-start.9 = (f32[8,128]{1,0:T(8,128)S(1)}, f32[8,128]{1,0:T(8,128)}, u32[]{:S(2)}) copy-start(f32[8,128]{1,0:T(8,128)} %get-tuple-element.20) | copy-start | bytes 12292
  95.0 1273.3 %copy-start.3 = (bf16[288,1024]{1,0:T(8,128)(2,1)S(1)}, bf16[288,1024]{1,0:T(8,128)(2,1)}, u32[]{:S(2)}) copy-start(bf16[288,1024]{1,0:T(8,128)(2,1)} %get-tuple-element.26) | copy-start | bytes 1769476
  95.1 1270.2 %all-to-all-start.2 = ((bf16[16,256,128]{2,1,0:T(8,128)(2,1)}), bf16[16,256,128]{2,1,0:T(8,128)(2,1)S(1)}, u32[]{:S(2)}, u32[]{:S(2)}) async-start(bf16[16,256,128]{2,1,0:T(8,128)(2,1)} %bitcast.8), calls=%async_computation.2 | async-start | bytes 2097152 | tf_op jit(solution)/shard_map/all_to_all | solution.py:454
  1365.3 1.0 copy-start
  1368.3 107.7 %copy-start.6 = (f32[8,1024]{1,0:T(8,128)S(1)}, f32[8,1024]{1,0:T(8,128)}, u32[]{:S(2)}) copy-start(f32[8,1024]{1,0:T(8,128)} %reduce-scatter.3.cloned.1.call-done) | copy-start | bytes 98308
  1368.4 107.7 %copy-start.7 = (f32[8,1024]{1,0:T(8,128)S(1)}, f32[8,1024]{1,0:T(8,128)}, u32[]{:S(2)}) copy-start(f32[8,1024]{1,0:T(8,128)} %reduce-scatter.5.cloned.1.call-done) | copy-start | bytes 98308
Sparse Core Ops, SparseCore 0:
  91.1 631.4 reduce-scatter.2
  725.1 638.7 reduce-scatter.4

commit v2 on v1

--- a/solution.py
+++ b/solution.py
@@ -28,13 +28,17 @@
     return pl.BlockSpec(memory_space=pltpu.VMEM)
 
 
+def anywhere():
+    return pl.BlockSpec(memory_space=pl.ANY)
+
+
 def smem():
     return pl.BlockSpec(memory_space=pltpu.SMEM)
 
 
 def pack_kernel(tile_ref, rows_ref, feats_ref, cells_ref, sfeats_ref, scells_ref, slot_ref, count):
     block_count, block_len = cells_ref.shape
-    tile_total = sfeats_ref.shape[0] // (CAP * block_len)
+    tile_total = scells_ref.shape[0]
     scells_ref[...] = jnp.full(scells_ref.shape, -1, jnp.int32)
     for t in range(tile_total):
         count[t] = 0
@@ -48,7 +52,7 @@
         sfeats_ref[pl.ds(pl.multiple_of(slot * block_len, block_len), block_len), :] = feats_ref[
             b * block_len : (b + 1) * block_len, :
         ]
-        scells_ref[pl.ds(slot, 1), :] = jnp.where(lane < rows_ref[b], cells_ref[b : b + 1, :], -1)
+        scells_ref[t, pl.ds(n, 1), :] = jnp.where(lane < rows_ref[b], cells_ref[b : b + 1, :], -1)
 
 
 def pack(block_tile, block_rows, radiances, row_cells, lat_count):
@@ -60,7 +64,7 @@
         pack_kernel,
         out_shape=(
             jax.ShapeDtypeStruct((slots * block_len, feat), BF16),
-            jax.ShapeDtypeStruct((slots, block_len), jnp.int32),
+            jax.ShapeDtypeStruct((lat_count, 8, block_len), jnp.int32),
             jax.ShapeDtypeStruct((block_count,), jnp.int32),
         ),
         in_specs=[smem(), smem(), vmem(), vmem()],
@@ -85,8 +89,7 @@
     wd_ref,
     lgrad_ref,
     rgrad_ref,
-    gq_ref,
-    go_ref,
+    gw_ref,
     gs_ref,
     loss_ref,
     comp,
@@ -112,7 +115,8 @@
     csem,
     osem,
 ):
-    slots, block_len = cells_ref.shape
+    sources, _, block_len = cells_ref.shape
+    slots = sources * CAP
     cells, width = lat_ref.shape
     feat = feats_ref.shape[1]
     disks_ch = disk_ref.shape[0]
@@ -125,7 +129,11 @@
     cw = ch * HEADS
     grid_rows = cells // 128
 
-    valid = (cells_ref[...] >= 0).astype(jnp.int32)
+    def place(s):
+        return (s // CAP) * 8 + s % CAP
+
+    got_cells = cells_ref[...].reshape(sources * 8, block_len)
+    valid = (got_cells >= 0).astype(jnp.int32)
     countv[...] = jnp.broadcast_to(jnp.sum(valid, axis=1, keepdims=True), countv.shape)
     copy = pltpu.make_async_copy(countv, counts, csem)
     copy.start()
@@ -190,18 +198,15 @@
     lax.fori_loop(0, cells // CHUNK, disk_mix, 0)
 
     copy.wait()
-    padded = jnp.concatenate(
-        [cells_ref[...], jnp.full((block_len - slots, block_len), -1, jnp.int32)], axis=0
-    )
-    columns = jnp.transpose(padded.astype(F32)).astype(jnp.int32)
+    columns = jnp.transpose(got_cells.astype(F32)).astype(jnp.int32)
     row = lax.broadcasted_iota(jnp.int32, (block_len, feat), 0)
     offset = jnp.int32(0)
     for s in range(slots):
         at = pl.ds(pl.multiple_of(offset, 16), block_len)
         got = feats_ref[s * block_len : (s + 1) * block_len, :]
-        comp[at, :] = jnp.where(row < counts[s, 0], got, jnp.zeros_like(got))
-        cellb[at, :] = jnp.broadcast_to(columns[:, s : s + 1], (block_len, 128))
-        offset = offset + ((counts[s, 0] + 15) // 16) * 16
+        comp[at, :] = jnp.where(row < counts[place(s), 0], got, jnp.zeros_like(got))
+        cellb[at, :] = jnp.broadcast_to(columns[:, place(s) : place(s) + 1], (block_len, 128))
+        offset = offset + ((counts[place(s), 0] + 15) // 16) * 16
     chunk_total = (offset + (CHUNK - 1)) // CHUNK
 
     lane = lax.broadcasted_iota(jnp.int32, (CHUNK, 128), 1)
@@ -224,7 +229,9 @@
         kv[r, :] = low
         oh = one_hot(r)
         q = mm(oh, query[...]).astype(BF16)
-        qr[r, :] = q
+        qr[pl.ds(pl.multiple_of(i * (CHUNK // 16), CHUNK // 16), CHUNK // 16)] = q.reshape(
+            CHUNK // 16, 16, width
+        )
         g = jax.nn.sigmoid(mm(q * low[:, :width], hsum[...]) * scale)
         gate[r, :] = g
         term = mm(g.astype(BF16), hspread[...]).astype(BF16) * low[:, width:]
@@ -266,8 +273,13 @@
         full = jnp.where(head_mask, mm(left, right, TN), 0.0)
         return jnp.sum(full.reshape(ch, HEADS, width), axis=1)
 
-    gs_ref[2 * feat : 2 * feat + ch, :] = disk_weight(ndisk, query[...]).astype(gs_ref.dtype)
-    gs_ref[2 * feat + ch :, :] = disk_weight(mdisk[...], gmix[...]).astype(gs_ref.dtype)
+    def small_out(at, value):
+        low = value.astype(gs_ref.dtype)
+        for j in range(gs_ref.shape[0]):
+            gs_ref[j, at : at + value.shape[0], :] = low[:, j * 128 : (j + 1) * 128]
+
+    small_out(2 * feat, disk_weight(ndisk, query[...]))
+    small_out(2 * feat + ch, disk_weight(mdisk[...], gmix[...]))
     mdisk[...] = ndisk
 
     def disk_query(i, _):
@@ -287,23 +299,24 @@
         ds_wide = mm(ds.astype(BF16), hspread[...]).astype(BF16)
         acc[...] += mm(oh, ds_wide * kv[r, :width], TN)
         g_wide = mm(g.astype(BF16), hspread[...]).astype(BF16)
-        grads = jnp.concatenate([ds_wide * qr[r, :], g_wide * gm], axis=1)
+        q = qr[pl.ds(pl.multiple_of(i * (CHUNK // 16), CHUNK // 16), CHUNK // 16)]
+        grads = jnp.concatenate([ds_wide * q.reshape(CHUNK, width), g_wide * gm], axis=1)
         gkv[...] += mm(comp[r, :], grads, TN)
         comp[r, :] = mm(grads, wkv_ref[...], NT).astype(BF16)
         return 0
 
     lax.fori_loop(0, chunk_total, backward, 0)
-    gs_ref[:feat, :] = gkv[:, :width].astype(gs_ref.dtype)
-    gs_ref[feat : 2 * feat, :] = gkv[:, width:].astype(gs_ref.dtype)
+    small_out(0, gkv[:, :width])
+    small_out(feat, gkv[:, width:])
 
     offset = jnp.int32(0)
     for s in range(slots):
         at = pl.ds(pl.multiple_of(offset, 16), block_len)
         got = comp[at, :]
         rgrad_ref[s * block_len : (s + 1) * block_len, :] = jnp.where(
-            row < counts[s, 0], got, jnp.zeros_like(got)
-        )
-        offset = offset + ((counts[s, 0] + 15) // 16) * 16
+            row < counts[place(s), 0], got, jnp.zeros_like(got)
+        )
+        offset = offset + ((counts[place(s), 0] + 15) // 16) * 16
 
     def finish(i, _):
         r = pl.ds(pl.multiple_of(i * tile, tile), tile)
@@ -314,48 +327,51 @@
 
     lax.fori_loop(0, cells // tile, finish, 0)
 
+    half = gw_ref.shape[1] // 2
+    slabs = CHUNK // half
+
+    def out_copy(i):
+        part = pl.ds(pl.multiple_of(i * slabs, slabs), slabs)
+        return pltpu.make_async_copy(stage.at[part], gw_ref.at[part], osem.at[i])
+
     def weights(i, _):
-        at = pl.multiple_of(i * CHUNK, CHUNK)
-        c = pl.ds(at, CHUNK)
-        later = pl.ds(pl.multiple_of(width + i * CHUNK, CHUNK), CHUNK)
-        qr[c, :] = mm(lat_ref[:, c], query[...], TN).astype(BF16)
-        pltpu.make_async_copy(qr.at[c], gq_ref.at[c], osem.at[0, i]).start()
-        qr[later, :] = mm(mixed[:, c], gul[...], TN).astype(BF16)
-        pltpu.make_async_copy(qr.at[later], go_ref.at[c], osem.at[1, i]).start()
+        c = pl.ds(pl.multiple_of(i * CHUNK, CHUNK), CHUNK)
+        gq = mm(lat_ref[:, c], query[...], TN).reshape(slabs, half, width)
+        go = mm(mixed[:, c], gul[...], TN).reshape(slabs, half, width)
+        part = pl.ds(pl.multiple_of(i * slabs, slabs), slabs)
+        stage[part] = jnp.concatenate([gq, go], axis=1).astype(BF16)
+        out_copy(i).start()
         return 0
 
+    stage = qr.at[: gw_ref.shape[0]]
     lax.fori_loop(0, width // CHUNK, weights, 0)
     for i in range(width // CHUNK):
-        c = slice(i * CHUNK, (i + 1) * CHUNK)
-        later = slice(width + i * CHUNK, width + (i + 1) * CHUNK)
-        pltpu.make_async_copy(qr.at[c], gq_ref.at[c], osem.at[0, i]).wait()
-        pltpu.make_async_copy(qr.at[later], go_ref.at[c], osem.at[1, i]).wait()
-
-
-def tile_step(weight, feats, cells, lat_flat, disk, target, wq, wkv, wdk, wdv, wo, wd):
+        out_copy(i).wait()
+
+
+def tile_step(devices, weight, feats, cells, lat_flat, disk, target, wq, wkv, wdk, wdv, wo, wd):
     rows, feat = feats.shape
     cell_count, width = lat_flat.shape
     ch = wdk.shape[0]
     disks = disk.shape[0] // ch
     cw = ch * HEADS
-    slots = cells.shape[0]
+    sources = cells.shape[0]
     return pl.pallas_call(
         tile_kernel,
         out_shape=(
             jax.ShapeDtypeStruct((cell_count, width), F32),
             jax.ShapeDtypeStruct((rows, feat), BF16),
-            jax.ShapeDtypeStruct((width, width), BF16),
-            jax.ShapeDtypeStruct((width, width), BF16),
-            jax.ShapeDtypeStruct((2 * feat + 2 * ch, width), BF16),
+            jax.ShapeDtypeStruct((devices, 2 * width // devices, width), BF16),
+            jax.ShapeDtypeStruct((width // 128, 2 * feat + 2 * ch, 128), BF16),
             jax.ShapeDtypeStruct((8, target.shape[1]), F32),
         ),
         in_specs=[smem()] + [vmem()] * 11,
-        out_specs=(vmem(), vmem(), pl.BlockSpec(memory_space=pl.ANY), pl.BlockSpec(memory_space=pl.ANY), vmem(), vmem()),
+        out_specs=(vmem(), vmem(), anywhere(), vmem(), vmem()),
         scratch_shapes=[
             pltpu.VMEM((rows, feat), BF16),
             pltpu.VMEM((rows, 128), jnp.int32),
             pltpu.VMEM((rows, 2 * width), BF16),
-            pltpu.VMEM((rows, width), BF16),
+            pltpu.VMEM((rows // 16, 16, width), BF16),
             pltpu.VMEM((rows, 128), F32),
             pltpu.VMEM((cell_count, width), F32),
             pltpu.VMEM((feat, 2 * width), F32),
@@ -370,33 +386,534 @@
             pltpu.VMEM((cell_count, cw), BF16),
             pltpu.VMEM((width, 128), BF16),
             pltpu.VMEM((128, width), BF16),
-            pltpu.VMEM((slots, 128), jnp.int32),
-            pltpu.SMEM((slots, 128), jnp.int32),
+            pltpu.VMEM((8 * sources, 128), jnp.int32),
+            pltpu.SMEM((8 * sources, 128), jnp.int32),
             pltpu.SemaphoreType.DMA,
-            pltpu.SemaphoreType.DMA((2, width // CHUNK)),
+            pltpu.SemaphoreType.DMA((width // CHUNK,)),
         ],
         compiler_params=pltpu.CompilerParams(vmem_limit_bytes=62 * 1024 * 1024),
         name="tile",
     )(weight, feats, cells, lat_flat, disk, target, wq, wkv, wdk, wdv, wo, wd)
 
 
-def unpack_kernel(slot_ref, got_ref, out_ref):
+SIDE = 4
+
+
+def lat_peer(p, k):
+    y = lax.rem(p // SIDE + k // SIDE, SIDE)
+    z = lax.rem(p % SIDE + k % SIDE, SIDE)
+    return y * SIDE + z
+
+
+def loop(count, step, start=0):
+    def run(i, carry):
+        step(i)
+        return carry
+
+    lax.fori_loop(start, count, run, 0)
+
+
+def send_kernel(feats_ref, cells_ref, got_ref, gcells_ref, fsend, frecv, csend, crecv, local):
+    lats = cells_ref.shape[0]
+    p = lax.axis_index("lat")
+    barrier = pltpu.get_barrier_semaphore()
+
+    def greet(k):
+        pl.semaphore_signal(
+            barrier, inc=1, device_id={"lat": lat_peer(p, k)}, device_id_type=pl.DeviceIdType.MESH
+        )
+
+    loop(lats, greet, 1)
+    own = pltpu.make_async_copy(feats_ref.at[p], got_ref.at[p], local.at[0])
+    own.start()
+    own_cells = pltpu.make_async_copy(cells_ref.at[p], gcells_ref.at[p], local.at[1])
+    own_cells.start()
+    pl.semaphore_wait(barrier, lats - 1)
+
+    def feats_copy(k):
+        to = lat_peer(p, k)
+        return pltpu.make_async_remote_copy(
+            src_ref=feats_ref.at[to],
+            dst_ref=got_ref.at[p],
+            send_sem=fsend.at[k],
+            recv_sem=frecv.at[k],
+            device_id={"lat": to},
+            device_id_type=pl.DeviceIdType.MESH,
+        )
+
+    def cells_copy(k):
+        to = lat_peer(p, k)
+        return pltpu.make_async_remote_copy(
+            src_ref=cells_ref.at[to],
+            dst_ref=gcells_ref.at[p],
+            send_sem=csend.at[k],
+            recv_sem=crecv.at[k],
+            device_id={"lat": to},
+            device_id_type=pl.DeviceIdType.MESH,
+        )
+
+    def begin(k):
+        feats_copy(k).start()
+        cells_copy(k).start()
+
+    def end(k):
+        feats_copy(k).wait()
+        cells_copy(k).wait()
+
+    loop(lats, begin, 1)
+    own.wait()
+    own_cells.wait()
+    loop(lats, end, 1)
+
+
+def send_rows(feats, cells):
+    lats = cells.shape[0]
+    dma = pltpu.SemaphoreType.DMA
+    return pl.pallas_call(
+        send_kernel,
+        out_shape=(
+            jax.ShapeDtypeStruct(feats.shape, feats.dtype),
+            jax.ShapeDtypeStruct(cells.shape, cells.dtype),
+        ),
+        in_specs=[anywhere(), anywhere()],
+        out_specs=(anywhere(), anywhere()),
+        scratch_shapes=[dma((lats,))] * 4 + [dma((2,))],
+        compiler_params=pltpu.CompilerParams(collective_id=1, has_side_effects=True),
+        name="send_rows",
+    )(feats, cells)
+
+
+def reduce_kernel(
+    wide_a,
+    gw_ref,
+    gs_ref,
+    loss_ref,
+    rgrad_ref,
+    share_ref,
+    small_ref,
+    stat_ref,
+    back_ref,
+    s1,
+    r1,
+    sg1,
+    rg1,
+    s2a,
+    r2a,
+    s2b,
+    r2b,
+    sg2,
+    rg2,
+    r3a,
+    r3b,
+    rg3,
+    sg3,
+    g4,
+    t4,
+    t5,
+    mine,
+    plane,
+    local,
+    s_core,
+    r_core,
+    s_back,
+    r_back,
+    s_a2,
+    r_a2,
+    s_g2,
+    r_g2,
+    s_b2,
+    r_b2,
+    s_a3,
+    r_a3,
+    s_b3,
+    r_b3,
+    s_g3,
+    r_g3,
+    s_g4,
+    r_g4,
+    s_t4,
+    r_t4,
+    s_g5,
+    r_g5,
+    s_t5,
+    r_t5,
+):
+    xs, cores, lats, slab, width = gw_ref.shape
+    lons = xs * cores
+    lon = lax.axis_index("lon")
+    p = lax.axis_index("lat")
+    x, c = lon // cores, lon % cores
+    other = 1 - c
+    rest = pl.ds(wide_a, width - wide_a)
+    first = pl.ds(0, wide_a)
+    piece = g4.shape[1]
+    pieces = small_ref.shape[1]
+    blocks = lats // SIDE
+
+    def to_lon(target, src, dst, ssem, rsem):
+        return pltpu.make_async_remote_copy(
+            src_ref=src,
+            dst_ref=dst,
+            send_sem=ssem,
+            recv_sem=rsem,
+            device_id={"lon": target},
+            device_id_type=pl.DeviceIdType.MESH,
+        )
+
+    def to_lat(target, src, dst, ssem, rsem):
+        return pltpu.make_async_remote_copy(
+            src_ref=src,
+            dst_ref=dst,
+            send_sem=ssem,
+            recv_sem=rsem,
+            device_id={"lat": target},
+            device_id_type=pl.DeviceIdType.MESH,
+        )
+
+    def x_peer(k):
+        return lax.rem(x + k, xs)
+
+    barrier = pltpu.get_barrier_semaphore()
+
+    def greet_lat(k):
+        pl.semaphore_signal(
+            barrier, inc=1, device_id={"lat": lat_peer(p, k)}, device_id_type=pl.DeviceIdType.MESH
+        )
+
+    def greet_lon(k):
+        pl.semaphore_signal(
+            barrier, inc=1, device_id={"lon": lax.rem(lon + k, lons)}, device_id_type=pl.DeviceIdType.MESH
+        )
+
+    loop(lats, greet_lat, 1)
+    loop(lons, greet_lon, 1)
+
+    def own_copy(j):
+        return pltpu.make_async_copy(gw_ref.at[j, c], s1.at[j], local.at[j])
+
+    loop(xs, lambda j: own_copy(j).start())
+    own_small = pltpu.make_async_copy(gs_ref.at[:, c], sg1, local.at[xs])
+    own_small.start()
+    own_back = pltpu.make_async_copy(rgrad_ref.at[p], back_ref.at[p], local.at[xs + 1])
+    own_back.start()
+    pl.semaphore_wait(barrier, lats + lons - 2)
+
+    mate = x * cores + other
+
+    def core_copy(k):
+        j = x_peer(k)
+        return to_lon(mate, gw_ref.at[j, other], r1.at[j], s_core.at[k], r_core.at[k])
+
+    core_small = to_lon(mate, gs_ref.at[:, other], rg1, s_core.at[xs], r_core.at[xs])
+    loop(xs, lambda k: core_copy(k).start(), 1)
+    core_small.start()
+    core_copy(0).start()
+
+    def back_copy(k):
+        to = lat_peer(p, k)
+        return to_lat(to, rgrad_ref.at[to], back_ref.at[p], s_back.at[k], r_back.at[k])
+
+    loop(lats, lambda k: back_copy(k).start(), 1)
+
+    def a2_copy(k):
+        j = x_peer(k)
+        return to_lon(
+            j * cores + c, s1.at[j, :, :, first], r2a.at[k - 1], s_a2.at[k], r_a2.at[k]
+        )
+
+    def g2_copy(k):
+        j = x_peer(k)
+        return to_lon(j * cores + c, sg1.at[j], rg2.at[k - 1], s_g2.at[k], r_g2.at[k])
+
+    def b2_copy(k):
+        to = lat_peer(p, k)
+        return to_lat(to, s1.at[:, to, :, rest], r2b.at[k - 1], s_b2.at[k], r_b2.at[k])
+
+    def add_core(j):
+        def step(i):
+            at = pl.ds(i * SIDE, SIDE)
+            s1[j, at] = s1[j, at] + r1[j, at]
+
+        loop(blocks, step)
+
+    def core_step(k):
+        j = x_peer(k)
+        own_copy(j).wait()
+        core_copy(k).wait_recv()
+        add_core(j)
+        a2_copy(k).start()
+
+    loop(xs, core_step, 1)
+    own_small.wait()
+    core_small.wait_recv()
+    sg1[...] = sg1[...] + rg1[...]
+    loop(xs, lambda k: g2_copy(k).start(), 1)
+    own_copy(x).wait()
+    core_copy(0).wait_recv()
+    add_core(x)
+    loop(lats, lambda k: b2_copy(k).start(), 1)
+
+    loop(xs, lambda k: a2_copy(k).wait_recv(), 1)
+    loop(xs, lambda k: g2_copy(k).wait_recv(), 1)
+
+    def a3_copy(k):
+        to = lat_peer(p, k)
+        return to_lat(to, s2a.at[to], r3a.at[k - 1], s_a3.at[k], r_a3.at[k])
+
+    def g3_copy(k):
+        to = lat_peer(p, k)
+        return to_lat(to, sg2.at[to], rg3.at[k - 1], s_g3.at[k], r_g3.at[k])
+
+    def b3_copy(k):
+        j = x_peer(k)
+        return to_lon(j * cores + c, s2b.at[j], r3b.at[k - 1], s_b3.at[k], r_b3.at[k])
+
+    total = sg1[x].astype(F32)
+    for k in range(xs - 1):
+        total = total + rg2[k].astype(F32)
+    sg2[...] = jnp.zeros(sg2.shape, BF16)
+    sg2[:pieces] = total.astype(BF16).reshape(pieces, piece, total.shape[1])
+
+    def sum_a(i):
+        value = s1[x, i, :, :wide_a].astype(F32)
+        for k in range(xs - 1):
+            value = value + r2a[k, i].astype(F32)
+        s2a[i] = value.astype(BF16)
+
+    loop(lats, sum_a)
+    loop(lats, lambda k: a3_copy(k).start(), 1)
+    loop(lats, lambda k: g3_copy(k).start(), 1)
+    loop(lats, lambda k: b2_copy(k).wait_recv(), 1)
+
+    def sum_b(j):
+        def add(k, value):
+            return value + r2b[k, j].astype(F32)
+
+        s2b[j] = lax.fori_loop(0, lats - 1, add, s1[j, p, :, wide_a:].astype(F32)).astype(BF16)
+
+    loop(xs, sum_b)
+    loop(xs, lambda k: b3_copy(k).start(), 1)
+
+    loop(lats, lambda k: g3_copy(k).wait_recv(), 1)
+
+    def add_small(k, value):
+        return value + rg3[k].astype(F32)
+
+    sg3[...] = lax.fori_loop(0, lats - 1, add_small, sg2[p].astype(F32)).astype(BF16)
+    g4[p] = sg3[...]
+
+    def g4_copy(k):
+        return to_lat(lat_peer(p, k), sg3, g4.at[p], s_g4.at[k], r_g4.at[k])
+
+    loop(lats, lambda k: g4_copy(k).start(), 1)
+    loop(lats, lambda k: a3_copy(k).wait_recv(), 1)
+
+    def add_share(k, value):
+        return value + r3a[k].astype(F32)
+
+    share_a = lax.fori_loop(0, lats - 1, add_share, s2a[p].astype(F32))
+    loop(xs, lambda k: b3_copy(k).wait_recv(), 1)
+    share_b = s2b[x].astype(F32)
+    for k in range(xs - 1):
+        share_b = share_b + r3b[k].astype(F32)
+    share_ref[:, :wide_a] = share_a
+    share_ref[:, wide_a:] = share_b
+    half = slab // 2
+
+    def lane_sums(value):
+        value = jnp.sum(value, axis=0, keepdims=True)
+        total = value[:, :128]
+        for j in range(1, value.shape[1] // 128):
+            total = total + value[:, j * 128 : (j + 1) * 128]
+        return total
+
+    square = jnp.concatenate([share_a * share_a, share_b * share_b], axis=1)
+    row = lax.broadcasted_iota(jnp.int32, mine.shape, 0)
+    mine[...] = jnp.where(
+        row == 0,
+        lane_sums(loss_ref[...]),
+        jnp.where(
+            row == 1,
+            lane_sums(square[:half]),
+            jnp.where(row == 2, lane_sums(square[half:]), 0.0),
+        ),
+    )
+
+    def t4_copy(k):
+        return to_lat(lat_peer(p, k), mine, t4.at[k - 1], s_t4.at[k], r_t4.at[k])
+
+    loop(lats, lambda k: t4_copy(k).start(), 1)
+
+    loop(lats, lambda k: g4_copy(k).wait_recv(), 1)
+
+    def g5_copy(k):
+        return to_lon(
+            lax.rem(lon + k, lons), g4.at[pl.ds(0, pieces)], small_ref.at[lon], s_g5.at[k], r_g5.at[k]
+        )
+
+    loop(lons, lambda k: g5_copy(k).start(), 1)
+    small_ref[lon] = g4[:pieces]
+    loop(lats, lambda k: t4_copy(k).wait_recv(), 1)
+    plane[...] = lax.fori_loop(0, lats - 1, lambda k, value: value + t4[k], mine[...])
+
+    def t5_copy(k):
+        return to_lon(lax.rem(lon + k, lons), plane, t5.at[k - 1], s_t5.at[k], r_t5.at[k])
+
+    loop(lons, lambda k: t5_copy(k).start(), 1)
+    loop(lons, lambda k: t5_copy(k).wait_recv(), 1)
+    stat_ref[...] = lax.fori_loop(0, lons - 1, lambda k, value: value + t5[k], plane[...])
+    loop(lons, lambda k: g5_copy(k).wait_recv(), 1)
+    own_back.wait()
+    loop(lats, lambda k: back_copy(k).wait_recv(), 1)
+
+    loop(xs, lambda k: core_copy(k).wait_send())
+    core_small.wait_send()
+
+    def sent_x(k):
+        a2_copy(k).wait_send()
+        g2_copy(k).wait_send()
+        b3_copy(k).wait_send()
+
+    loop(xs, sent_x, 1)
+
+    def sent_lat(k):
+        back_copy(k).wait_send()
+        b2_copy(k).wait_send()
+        a3_copy(k).wait_send()
+        g3_copy(k).wait_send()
+        g4_copy(k).wait_send()
+        t4_copy(k).wait_send()
+
+    loop(lats, sent_lat, 1)
+
+    def sent_lon(k):
+        g5_copy(k).wait_send()
+        t5_copy(k).wait_send()
+
+    loop(lons, sent_lon, 1)
+
+
+def reduce_all(gw, gs, loss, rgrad):
+    xs, cores, lats, slab, width = gw.shape
+    lons = xs * cores
+    small_rows = gs.shape[2]
+    piece = 32
+    pieces = small_rows // piece
+    wide_a = 640
+    wide_b = width - wide_a
+    dma = pltpu.SemaphoreType.DMA
+
+    def buf(*shape, dtype=BF16):
+        return pltpu.VMEM(shape, dtype)
+
+    pairs = [xs + 1, lats, xs, xs, lats, lats, xs, lats, lats, lats, lons, lons]
+    return pl.pallas_call(
+        functools.partial(reduce_kernel, wide_a),
+        out_shape=(
+            jax.ShapeDtypeStruct((slab, width), F32),
+            jax.ShapeDtypeStruct((lons, pieces, piece, 128), BF16),
+            jax.ShapeDtypeStruct((8, 128), F32),
+            jax.ShapeDtypeStruct(rgrad.shape, BF16),
+        ),
+        in_specs=[anywhere(), vmem(), vmem(), anywhere()],
+        out_specs=(vmem(), vmem(), vmem(), anywhere()),
+        scratch_shapes=[
+            buf(xs, lats, slab, width),
+            buf(xs, lats, slab, width),
+            buf(xs, small_rows, 128),
+            buf(xs, small_rows, 128),
+            buf(lats, slab, wide_a),
+            buf(xs - 1, lats, slab, wide_a),
+            buf(xs, slab, wide_b),
+            buf(lats - 1, xs, slab, wide_b),
+            buf(lats, piece, 128),
+            buf(xs - 1, small_rows, 128),
+            buf(lats - 1, slab, wide_a),
+            buf(xs - 1, slab, wide_b),
+            buf(lats - 1, piece, 128),
+            buf(piece, 128),
+            buf(lats, piece, 128),
+            buf(lats - 1, 8, 128, dtype=F32),
+            buf(lons - 1, 8, 128, dtype=F32),
+            buf(8, 128, dtype=F32),
+            buf(8, 128, dtype=F32),
+            dma((xs + 2,)),
+        ]
+        + [dma((n,)) for n in pairs for _ in range(2)],
+        compiler_params=pltpu.CompilerParams(
+            collective_id=2, has_side_effects=True, vmem_limit_bytes=40 * 1024 * 1024
+        ),
+        name="reduce_all",
+    )(gw, gs, loss, rgrad)
+
+
+def finish_kernel(
+    loss_scale,
+    slot_ref,
+    got_ref,
+    share_ref,
+    small_ref,
+    stat_ref,
+    out_ref,
+    query_ref,
+    wout_ref,
+    key_ref,
+    value_ref,
+    dkey_ref,
+    dvalue_ref,
+    loss_ref,
+):
     block_count = slot_ref.shape[0]
     block_len = out_ref.shape[0] // block_count
+    half, width = query_ref.shape
     for b in range(block_count):
         out_ref[b * block_len : (b + 1) * block_len, :] = got_ref[
             pl.ds(pl.multiple_of(slot_ref[b] * block_len, block_len), block_len), :
         ]
 
-
-def unpack(slots, got, rows):
+    loss_ref[...] = jnp.sum(stat_ref[0:1, :], axis=1, keepdims=True) * loss_scale
+
+    def scale(total, entries):
+        return 1.0 / jnp.sqrt(total / entries + 1e-06)
+
+    def whole(value):
+        return jnp.sum(jnp.sum(value, axis=0, keepdims=True), axis=1, keepdims=True)
+
+    query_ref[...] = share_ref[:half] * scale(whole(stat_ref[1:2, :]), width * width)
+    wout_ref[...] = share_ref[half:] * scale(whole(stat_ref[2:3, :]), width * width)
+    lons, pieces, piece, lanes = small_ref.shape
+    sums = jnp.concatenate(
+        [small_ref[j].reshape(pieces * piece, lanes).astype(F32) for j in range(lons)], axis=1
+    )
+    at = 0
+    for ref in (key_ref, value_ref, dkey_ref, dvalue_ref):
+        n = ref.shape[0]
+        g = sums[at : at + n]
+        ref[...] = g * scale(whole(g * g), n * width)
+        at += n
+
+
+def finish(loss_scale, slots, got, share, small, stat, rows, feat, ch):
+    width = share.shape[1]
+    half = share.shape[0] // 2
+    shapes = [
+        ((rows, got.shape[1]), BF16),
+        ((half, width), F32),
+        ((half, width), F32),
+        ((feat, width), F32),
+        ((feat, width), F32),
+        ((ch, width), F32),
+        ((ch, width), F32),
+        ((1, 1), F32),
+    ]
     return pl.pallas_call(
-        unpack_kernel,
-        out_shape=jax.ShapeDtypeStruct((rows, got.shape[1]), BF16),
-        in_specs=[smem(), vmem()],
-        out_specs=vmem(),
-        name="unpack",
-    )(slots, got)
+        functools.partial(finish_kernel, loss_scale),
+        out_shape=tuple(jax.ShapeDtypeStruct(s, d) for s, d in shapes),
+        in_specs=[smem()] + [vmem()] * 4,
+        out_specs=(vmem(),) * len(shapes),
+        compiler_params=pltpu.CompilerParams(vmem_limit_bytes=32 * 1024 * 1024),
+        name="finish",
+    )(slots, got, share, small, stat)
 
 
 def cell_weights(row_total):
@@ -430,16 +947,12 @@
     feat = radiances.shape[1]
     ch = w_disk_key.shape[0]
     sfeats, scells, slot = pack(block_tile, block_rows, radiances, row_cells, lat_count)
-    got_feats = lax.all_to_all(
-        sfeats.reshape(lat_count, -1, feat), "lat", split_axis=0, concat_axis=0, tiled=True
-    ).reshape(sfeats.shape)
-    got_cells = lax.all_to_all(
-        scells.reshape(lat_count, CAP, -1), "lat", split_axis=0, concat_axis=0, tiled=True
-    ).reshape(scells.shape)
+    got_feats, got_cells = send_rows(sfeats.reshape(lat_count, -1, feat), scells)
     weight = jnp.asarray(cell_weights(tile_lat * lat_count))
-    lgrad, rgrad, gq, go, gs, loss = tile_step(
+    lgrad, rgrad, gw, gs, loss = tile_step(
+        device_count,
         weight,
-        got_feats,
+        got_feats.reshape(-1, feat),
         got_cells,
         latents.reshape(cells, width),
         disk_pixels.reshape(-1, cells),
@@ -451,36 +964,35 @@
         w_out,
         w_decode,
     )
-    returned = lax.all_to_all(
-        rgrad.reshape(lat_count, -1, feat), "lat", split_axis=0, concat_axis=0, tiled=True
-    ).reshape(rgrad.shape)
-    row_grad = unpack(slot, returned, rows)
-    axes = ("lon", "lat")
-    gq_share = lax.psum_scatter(gq.astype(F32), axes, scatter_dimension=0, tiled=True)
-    go_share = lax.psum_scatter(go.astype(F32), axes, scatter_dimension=0, tiled=True)
-    gs_sum, loss_sum, sq, so = lax.psum(
-        (
-            gs.astype(F32),
-            jnp.sum(loss),
-            jnp.sum(gq_share * gq_share),
-            jnp.sum(go_share * go_share),
-        ),
-        axes,
+    cores = 2
+    xs = lax.axis_size("lon") // cores
+    share, small, stat, returned = reduce_all(
+        gw.reshape((xs, cores, lat_count) + gw.shape[1:]),
+        gs.reshape((xs, cores) + gs.shape[1:]),
+        loss,
+        rgrad.reshape(lat_count, -1, feat),
     )
-    entries = width * width
-    small = []
-    at = 0
-    for n in (feat, feat, ch, ch):
-        g = gs_sum[at : at + n]
-        small.append(g / jnp.sqrt(jnp.mean(g * g) + 1e-06))
-        at += n
+    row_grad, query, out, key, value, dkey, dvalue, total = finish(
+        1.0 / (cells * device_count * out_width),
+        slot,
+        returned.reshape(-1, feat),
+        share,
+        small,
+        stat,
+        rows,
+        feat,
+        ch,
+    )
     return (
-        loss_sum * (1.0 / (cells * device_count * out_width)),
+        total.reshape(()),
         lgrad.reshape(latents.shape),
         row_grad,
-        gq_share / jnp.sqrt(sq / entries + 1e-06),
-        go_share / jnp.sqrt(so / entries + 1e-06),
-        *small,
+        query,
+        out,
+        key,
+        value,
+        dkey,
+        dvalue,
     )
 
 

time: 1490 us -> 148 us (0.10)
  waiting for transfers between devices: 1260 us -> 0 us
  blocking collectives: 115 us -> 0 us
  Pallas kernels: 47.2 us -> 138 us
  starting transfers between devices: 21.6 us -> 0 us
  between operations: 20.1 us -> 0.69 us
    reduce_scatter x2 -> x0, waiting for transfers between devices: 1250 us -> none  [the longest x1 640 us: body(): lax.psum_scatter(go.astype(F32), axes, scatter_dimension=0, tiled=True)]
    psum x1 -> x0, blocking collectives: 99.8 us -> none  [body(): lax.psum((gs.astype(F32), jnp.sum(loss), jnp.sum(gq_share * gq_share), jn...]
    pallas_call x1 -> x3, Pallas kernels: 2.06 us -> 74.1 us  [the longest x1 49.4 us: reduce_all(): pl.pallas_call(functools.partial(reduce_kernel, wide_a), out_shape=(jax.S...]
    all_to_all x2 -> x0, starting transfers between devices: 21.6 us -> none  [the longest x1 17.9 us: body(): lax.all_to_all(rgrad.reshape(lat_count, -1, feat), 'lat', split_axis=0, c...]
    pallas_call x1, Pallas kernels: 43 us -> 62.1 us  [tile_step(): pl.pallas_call(tile_kernel, out_shape=(jax.ShapeDtypeStruct((cell_count,...]
    all_to_all x1 -> x0, blocking collectives: 15.2 us -> none  [body(): lax.all_to_all(scells.reshape(lat_count, CAP, -1), 'lat', split_axis=0, c...]
  transfers between devices with their start and end apart: 4 -> 0, of which waited for: 3 -> 0; matrix products, arithmetic and copies ran while one was open for 0% -> 0% of each run, Pallas kernels for 0% -> 0%
where the time goes in v2:
time: 148 us
  Pallas kernels  138 us (93%)
  local copies, waits for them, and re-layouts  6.69 us (5%)
  other arithmetic  1.86 us (1%)
    pallas_call x1, Pallas kernels, tile_step(): pl.pallas_call(tile_kernel, out_shape=(jax.ShapeDtypeStruct((cell_count,...  62.1 us
    pallas_call x1, Pallas kernels, reduce_all(): pl.pallas_call(functools.partial(reduce_kernel, wide_a), out_shape=(jax.S...  49.4 us
    pallas_call x1, Pallas kernels, send_rows(): pl.pallas_call(send_kernel, out_shape=(jax.ShapeDtypeStruct(feats.shape,...  22.6 us
    unnamed x11, local copies, waits for them, and re-layouts  6.69 us

profile of v2, /device:TPU:1, one launch (start us, length us, event | category | flops | bytes accessed | tf_op | source)
XLA Modules:
  0.0 147.5 jit_solution(5029315442807851307)
XLA Ops:
  0.6 1.5 %copy.26 = bf16[10,8,4,128]{3,1,2,0:T(8,128)(2,1)} copy(bf16[10,8,4,128]{3,2,1,0:T(4,128)(2,1)} %bitcast.25) | data formatting | bytes 163840
  2.2 1.9 %pad_maximum_fusion.wkv_ref = bf16[128,2048]{1,0:T(8,128)(2,1)} fusion(bf16[128,1024]{1,0:T(8,128)(2,1)} %param.24, bf16[128,1024]{1,0:T(8,128)(2,1)} %param.23), kind=kLoop, calls=%fused_computation | loop fusion | flops 1048576 | bytes 1048576 | tf_op jit(solution)/shard_map/concatenate | solution.py:961
  4.0 2.1 %pack.1 = (bf16[4096,128]{1,0:T(8,128)(2,1)}, s32[16,8,128]{2,1,0:T(8,128)}, s32[16]{0:T(128)}) custom-call(s32[16]{0:T(128)} %tile_ref.1, s32[16]{0:T(128)} %rows_ref.1, bf16[2048,128]{1,0:T(8,128)(2,1)} %feats_ref.1, s32[16,128]{1,0:T(8,128)} %bitcast.26), custom_call_target="tpu_custom_call" | custom-call | tf_op jit(solution)/shard_map/pack/pallas_call | solution.py:63
  6.2 22.6 %send_rows.1 = (bf16[16,256,128]{2,1,0:T(8,128)(2,1)}, s32[16,8,128]{2,1,0:T(8,128)}) custom-call(bf16[16,256,128]{2,1,0:T(8,128)(2,1)} %bitcast.20, s32[16,8,128]{2,1,0:T(8,128)} %get-tuple-element.33.cells_ref), custom_call_target="tpu_custom_call" | custom-call | tf_op jit(solution)/shard_map/send_rows/pallas_call | solution.py:472
  28.8 62.1 %tile.1 = (f32[512,1024]{1,0:T(8,128)}, bf16[4096,128]{1,0:T(8,128)(2,1)}, bf16[128,16,1024]{2,1,0:T(8,128)(2,1)}, bf16[8,288,128]{2,1,0:T(8,128)(2,1)}, f32[8,128]{1,0:T(8,128)}) custom-call(f32[64]{0:T(128)} %constant.2.clone.weight_ref, bf16[4096,128]{1,0:T(8,128)(2,1)} %bitcast.22, s32[16,8,128]{2,1,0:T(8,128)} %get-tuple-element.35.cells_ref, ...), custom_call_target="tpu_custom_call" | custom-call | tf_op jit(solution)/shard_map/tile/pallas_call | solution.py:359
  90.9 0.0 copy-start
  90.9 2.2 %copy-done = bf16[128,16,1024]{2,1,0:T(8,128)(2,1)S(1)} copy-done((bf16[128,16,1024]{2,1,0:T(8,128)(2,1)S(1)}, bf16[128,16,1024]{2,1,0:T(8,128)(2,1)}, u32[]{:S(2)}) %copy-start) | copy-done | bytes 4194328
  93.1 0.0 copy-start.1
  93.1 1.2 copy-done.1
  94.3 0.0 copy-start.2
  94.3 1.1 copy-done.2
  95.4 0.0 copy-start.3
  95.4 0.7 copy-done.3
  96.1 0.0 copy-start.4
  96.1 49.4 %reduce_all.1 = (f32[16,1024]{1,0:T(8,128)S(1)}, bf16[8,9,32,128]{3,2,1,0:T(8,128)(2,1)S(1)}, f32[8,128]{1,0:T(8,128)S(1)}, bf16[16,256,128]{2,1,0:T(8,128)(2,1)S(1)}) custom-call(bf16[4,2,16,16,1024]{4,3,2,1,0:T(8,128)(2,1)S(1)} %bitcast.16, bf16[4,2,288,128]{3,2,1,0:T(8,128)(2,1)S(1)} %bitcast.19, f32[8,128]{1,0:T(8,128)S(1)} %copy-done.3, ...), custom_call_target="tpu_custom_call" | custom-call | tf_op jit(solution)/shard_map/reduce_all/pallas_call | solution.py:810
  145.5 0.0 copy-done.4
  145.5 2.0 %finish.1 = (bf16[2048,128]{1,0:T(8,128)(2,1)}, f32[8,1024]{1,0:T(8,128)}, f32[8,1024]{1,0:T(8,128)}, f32[128,1024]{1,0:T(8,128)}, f32[128,1024]{1,0:T(8,128)}, ...) custom-call(s32[16]{0:T(128)S(1)} %copy-done.4, bf16[4096,128]{1,0:T(8,128)(2,1)S(1)} %bitcast.18, ...), custom_call_target="tpu_custom_call" | custom-call | tf_op jit(solution)/shard_map/finish/pallas_call | solution.py:909
Async XLA Ops:
  90.9 2.2 %copy-start = (bf16[128,16,1024]{2,1,0:T(8,128)(2,1)S(1)}, bf16[128,16,1024]{2,1,0:T(8,128)(2,1)}, u32[]{:S(2)}) copy-start(bf16[128,16,1024]{2,1,0:T(8,128)(2,1)} %get-tuple-element.36) | copy-start | bytes 12582916
  93.1 1.2 copy-start.1
  94.3 1.1 copy-start.2
  95.4 0.7 copy-start.3
  96.1 49.5 %copy-start.4 = (s32[16]{0:T(128)S(1)}, s32[16]{0:T(128)}, u32[]{:S(2)}) copy-start(s32[16]{0:T(128)} %get-tuple-element.31.slot_ref) | copy-start | bytes 196

commit v3 on v2

--- a/solution.py
+++ b/solution.py
@@ -34,6 +34,22 @@
 
 def smem():
     return pl.BlockSpec(memory_space=pltpu.SMEM)
+
+
+def head_match(cw, width, hd):
+    return (
+        lax.broadcasted_iota(jnp.int32, (cw, width), 0) % HEADS
+        == lax.broadcasted_iota(jnp.int32, (cw, width), 1) // hd
+    )
+
+
+def channel_sum(cw, lanes):
+    return jnp.where(
+        lax.broadcasted_iota(jnp.int32, (cw, lanes), 0) % HEADS
+        == lax.broadcasted_iota(jnp.int32, (cw, lanes), 1),
+        1.0,
+        0.0,
+    ).astype(BF16)
 
 
 def pack_kernel(tile_ref, rows_ref, feats_ref, cells_ref, sfeats_ref, scells_ref, slot_ref, count):
@@ -79,15 +95,19 @@
     feats_ref,
     cells_ref,
     lat_ref,
-    disk_ref,
-    target_ref,
-    wq_ref,
-    wkv_ref,
-    wdk_ref,
-    wdv_ref,
-    wo_ref,
-    wd_ref,
-    lgrad_ref,
+    query,
+    px,
+    gdisk,
+    mdisk,
+    bkt,
+    bvt,
+    wk_ref,
+    wv_ref,
+    target_hbm,
+    wq_hbm,
+    wo_hbm,
+    wd_hbm,
+    lgrad_hbm,
     rgrad_ref,
     gw_ref,
     gs_ref,
@@ -99,38 +119,49 @@
     gate,
     acc,
     gkv,
-    query,
+    gquery,
     mixed,
     gul,
     gmix,
-    px,
-    bkt,
-    bvt,
-    gdisk,
-    mdisk,
+    ndisk,
+    target_ref,
+    wq_ref,
+    wo_ref,
+    wd_ref,
+    lgrad_ref,
     hsum,
     hspread,
     countv,
     counts,
     csem,
     osem,
+    isem,
+    lsem,
 ):
     sources, _, block_len = cells_ref.shape
     slots = sources * CAP
     cells, width = lat_ref.shape
     feat = feats_ref.shape[1]
-    disks_ch = disk_ref.shape[0]
-    ch = wdk_ref.shape[0]
-    disks = disks_ch // ch
+    cw = bkt.shape[0]
+    ch = cw // HEADS
+    disks = px.shape[1] // cw
     hd = width // HEADS
     scale = 1.0 / math.sqrt(hd)
     out_width = target_ref.shape[1]
     hl = hsum.shape[1]
-    cw = ch * HEADS
     grid_rows = cells // 128
 
     def place(s):
         return (s // CAP) * 8 + s % CAP
+
+    loads = [
+        pltpu.make_async_copy(hbm, held, isem.at[i])
+        for i, (hbm, held) in enumerate(
+            ((wo_hbm, wo_ref), (wd_hbm, wd_ref), (target_hbm, target_ref), (wq_hbm, wq_ref))
+        )
+    ]
+    for load in loads:
+        load.start()
 
     got_cells = cells_ref[...].reshape(sources * 8, block_len)
     valid = (got_cells >= 0).astype(jnp.int32)
@@ -153,43 +184,6 @@
     comp[...] = jnp.zeros(comp.shape, BF16)
     cellb[...] = jnp.full(cellb.shape, -1, jnp.int32)
 
-    def project(i, _):
-        r = pl.ds(pl.multiple_of(i * CHUNK, CHUNK), CHUNK)
-        query[r, :] = mm(lat_ref[r, :], wq_ref[...]).astype(BF16)
-        return 0
-
-    lax.fori_loop(0, cells // CHUNK, project, 0)
-
-    spread_ch = jnp.where(
-        lax.broadcasted_iota(jnp.int32, (cw, ch), 0) // HEADS
-        == lax.broadcasted_iota(jnp.int32, (cw, ch), 1),
-        1.0,
-        0.0,
-    ).astype(BF16)
-    head_mask = (
-        lax.broadcasted_iota(jnp.int32, (cw, width), 0) % HEADS
-        == lax.broadcasted_iota(jnp.int32, (cw, width), 1) // hd
-    )
-    bkt[...] = jnp.where(head_mask, mm(spread_ch, wdk_ref[...]), 0.0).astype(BF16)
-    bvt[...] = jnp.where(head_mask, mm(spread_ch, wdv_ref[...]), 0.0).astype(BF16)
-    sum_ch = jnp.where(
-        lax.broadcasted_iota(jnp.int32, (cw, hl), 0) % HEADS
-        == lax.broadcasted_iota(jnp.int32, (cw, hl), 1),
-        1.0,
-        0.0,
-    ).astype(BF16)
-    qt = mm(query[...], bkt[...], NT)
-    msum = jnp.zeros((cells, cw), F32)
-    for k in range(disks):
-        pxk = mm(
-            disk_ref[k * ch : (k + 1) * ch, :], spread_ch, (((0,), (1,)), ((), ()))
-        )
-        px[:, k * cw : (k + 1) * cw] = pxk.astype(BF16)
-        g = jax.nn.sigmoid(mm((pxk * qt).astype(BF16), sum_ch) * scale)
-        gdisk[:, k * hl : (k + 1) * hl] = g
-        msum = msum + mm(g.astype(BF16), sum_ch, NT) * pxk
-    mdisk[...] = msum.astype(BF16)
-
     def disk_mix(i, _):
         r = pl.ds(pl.multiple_of(i * CHUNK, CHUNK), CHUNK)
         acc[r, :] = mm(mdisk[r, :], bvt[...])
@@ -224,24 +218,28 @@
     def forward(i, _):
         r = pl.ds(pl.multiple_of(i * CHUNK, CHUNK), CHUNK)
         f = comp[r, :]
-        both = mm(f, wkv_ref[...])
-        low = both.astype(BF16)
-        kv[r, :] = low
+        key = mm(f, wk_ref[...]).astype(BF16)
+        value = mm(f, wv_ref[...]).astype(BF16)
+        kv[r, :width] = key
+        kv[r, width:] = value
         oh = one_hot(r)
         q = mm(oh, query[...]).astype(BF16)
         qr[pl.ds(pl.multiple_of(i * (CHUNK // 16), CHUNK // 16), CHUNK // 16)] = q.reshape(
             CHUNK // 16, 16, width
         )
-        g = jax.nn.sigmoid(mm(q * low[:, :width], hsum[...]) * scale)
+        g = jax.nn.sigmoid(mm(q * key, hsum[...]) * scale)
         gate[r, :] = g
-        term = mm(g.astype(BF16), hspread[...]).astype(BF16) * low[:, width:]
+        term = mm(g.astype(BF16), hspread[...]).astype(BF16) * value
         acc[...] += mm(oh, term, TN)
         return 0
 
     lax.fori_loop(0, chunk_total, forward, 0)
 
     lat_at = lax.axis_index("lat") * grid_rows
-    tile = 128
+    tile = CHUNK
+    lines = tile // 128
+    for load in loads[:3]:
+        load.wait()
 
     def middle(i, loss):
         r = pl.ds(pl.multiple_of(i * tile, tile), tile)
@@ -249,8 +247,10 @@
         mixed[r, :] = m
         updated = (lat_ref[r, :].astype(F32) + mm(m, wo_ref[...])).astype(BF16)
         err = mm(updated, wd_ref[...]) - target_ref[r, :]
-        w = weight_ref[lat_at + i]
-        gp = w * err
+        at = lat_at + i * lines
+        gp = jnp.concatenate(
+            [weight_ref[at + j] * err[j * 128 : (j + 1) * 128] for j in range(lines)], axis=0
+        )
         gu = mm(gp.astype(BF16), wd_ref[...], NT)
         lgrad_ref[r, :] = gu
         gu_low = gu.astype(BF16)
@@ -260,6 +260,8 @@
 
     loss_ref[...] = lax.fori_loop(0, cells // tile, middle, jnp.zeros((8, out_width), F32))
 
+    head_mask = head_match(cw, width, hd)
+    sum_ch = channel_sum(cw, hl)
     gt = mm(gmix[...], bvt[...], NT)
     nsum = jnp.zeros((cells, cw), F32)
     for k in range(disks):
@@ -267,7 +269,7 @@
         g = gdisk[:, k * hl : (k + 1) * hl]
         ds = mm((pxk * gt).astype(BF16), sum_ch) * g * (1.0 - g) * scale
         nsum = nsum + mm(ds.astype(BF16), sum_ch, NT) * pxk
-    ndisk = nsum.astype(BF16)
+    ndisk[...] = nsum.astype(BF16)
 
     def disk_weight(left, right):
         full = jnp.where(head_mask, mm(left, right, TN), 0.0)
@@ -278,13 +280,12 @@
         for j in range(gs_ref.shape[0]):
             gs_ref[j, at : at + value.shape[0], :] = low[:, j * 128 : (j + 1) * 128]
 
-    small_out(2 * feat, disk_weight(ndisk, query[...]))
+    small_out(2 * feat, disk_weight(ndisk[...], query[...]))
     small_out(2 * feat + ch, disk_weight(mdisk[...], gmix[...]))
-    mdisk[...] = ndisk
 
     def disk_query(i, _):
         r = pl.ds(pl.multiple_of(i * CHUNK, CHUNK), CHUNK)
-        acc[r, :] = mm(mdisk[r, :], bkt[...])
+        acc[r, :] = mm(ndisk[r, :], bkt[...])
         return 0
 
     lax.fori_loop(0, cells // CHUNK, disk_query, 0)
@@ -302,7 +303,8 @@
         q = qr[pl.ds(pl.multiple_of(i * (CHUNK // 16), CHUNK // 16), CHUNK // 16)]
         grads = jnp.concatenate([ds_wide * q.reshape(CHUNK, width), g_wide * gm], axis=1)
         gkv[...] += mm(comp[r, :], grads, TN)
-        comp[r, :] = mm(grads, wkv_ref[...], NT).astype(BF16)
+        back = mm(grads[:, :width], wk_ref[...], NT) + mm(grads[:, width:], wv_ref[...], NT)
+        comp[r, :] = back.astype(BF16)
         return 0
 
     lax.fori_loop(0, chunk_total, backward, 0)
@@ -318,11 +320,18 @@
         )
         offset = offset + ((counts[place(s), 0] + 15) // 16) * 16
 
+    loads[3].wait()
+
+    def lgrad_copy(i):
+        r = pl.ds(pl.multiple_of(i * tile, tile), tile)
+        return pltpu.make_async_copy(lgrad_ref.at[r], lgrad_hbm.at[r], lsem.at[i])
+
     def finish(i, _):
         r = pl.ds(pl.multiple_of(i * tile, tile), tile)
         gq = acc[r, :].astype(BF16)
-        query[r, :] = gq
+        gquery[r, :] = gq
         lgrad_ref[r, :] += mm(gq, wq_ref[...], NT)
+        lgrad_copy(i).start()
         return 0
 
     lax.fori_loop(0, cells // tile, finish, 0)
@@ -336,7 +345,7 @@
 
     def weights(i, _):
         c = pl.ds(pl.multiple_of(i * CHUNK, CHUNK), CHUNK)
-        gq = mm(lat_ref[:, c], query[...], TN).reshape(slabs, half, width)
+        gq = mm(lat_ref[:, c], gquery[...], TN).reshape(slabs, half, width)
         go = mm(mixed[:, c], gul[...], TN).reshape(slabs, half, width)
         part = pl.ds(pl.multiple_of(i * slabs, slabs), slabs)
         stage[part] = jnp.concatenate([gq, go], axis=1).astype(BF16)
@@ -347,14 +356,15 @@
     lax.fori_loop(0, width // CHUNK, weights, 0)
     for i in range(width // CHUNK):
         out_copy(i).wait()
-
-
-def tile_step(devices, weight, feats, cells, lat_flat, disk, target, wq, wkv, wdk, wdv, wo, wd):
+    for i in range(cells // tile):
+        lgrad_copy(i).wait()
+
+
+def tile_step(devices, weight, feats, cells, lat_flat, disk_state, wk, wv, target, wq, wo, wd):
     rows, feat = feats.shape
     cell_count, width = lat_flat.shape
-    ch = wdk.shape[0]
-    disks = disk.shape[0] // ch
-    cw = ch * HEADS
+    cw = disk_state[-1].shape[0]
+    ch = cw // HEADS
     sources = cells.shape[0]
     return pl.pallas_call(
         tile_kernel,
@@ -365,8 +375,8 @@
             jax.ShapeDtypeStruct((width // 128, 2 * feat + 2 * ch, 128), BF16),
             jax.ShapeDtypeStruct((8, target.shape[1]), F32),
         ),
-        in_specs=[smem()] + [vmem()] * 11,
-        out_specs=(vmem(), vmem(), anywhere(), vmem(), vmem()),
+        in_specs=[smem()] + [vmem()] * 11 + [anywhere()] * 4,
+        out_specs=(anywhere(), vmem(), anywhere(), vmem(), vmem()),
         scratch_shapes=[
             pltpu.VMEM((rows, feat), BF16),
             pltpu.VMEM((rows, 128), jnp.int32),
@@ -379,21 +389,24 @@
             pltpu.VMEM((cell_count, width), BF16),
             pltpu.VMEM((cell_count, width), BF16),
             pltpu.VMEM((cell_count, width), BF16),
-            pltpu.VMEM((cell_count, disks * cw), BF16),
-            pltpu.VMEM((cw, width), BF16),
-            pltpu.VMEM((cw, width), BF16),
-            pltpu.VMEM((cell_count, disks * 128), F32),
             pltpu.VMEM((cell_count, cw), BF16),
+            pltpu.VMEM(target.shape, F32),
+            pltpu.VMEM(wq.shape, BF16),
+            pltpu.VMEM(wo.shape, BF16),
+            pltpu.VMEM(wd.shape, BF16),
+            pltpu.VMEM((cell_count, width), F32),
             pltpu.VMEM((width, 128), BF16),
             pltpu.VMEM((128, width), BF16),
             pltpu.VMEM((8 * sources, 128), jnp.int32),
             pltpu.SMEM((8 * sources, 128), jnp.int32),
             pltpu.SemaphoreType.DMA,
             pltpu.SemaphoreType.DMA((width // CHUNK,)),
+            pltpu.SemaphoreType.DMA((4,)),
+            pltpu.SemaphoreType.DMA((cell_count // CHUNK,)),
         ],
         compiler_params=pltpu.CompilerParams(vmem_limit_bytes=62 * 1024 * 1024),
         name="tile",
-    )(weight, feats, cells, lat_flat, disk, target, wq, wkv, wdk, wdv, wo, wd)
+    )(weight, feats, cells, lat_flat, *disk_state, wk, wv, target, wq, wo, wd)
 
 
 SIDE = 4
@@ -413,7 +426,28 @@
     lax.fori_loop(start, count, run, 0)
 
 
-def send_kernel(feats_ref, cells_ref, got_ref, gcells_ref, fsend, frecv, csend, crecv, local):
+def send_kernel(
+    feats_ref,
+    cells_ref,
+    lat_ref,
+    disk_ref,
+    wdk_ref,
+    wdv_ref,
+    wq_ref,
+    got_ref,
+    gcells_ref,
+    query,
+    px,
+    gdisk,
+    mdisk,
+    bkt,
+    bvt,
+    fsend,
+    frecv,
+    csend,
+    crecv,
+    local,
+):
     lats = cells_ref.shape[0]
     p = lax.axis_index("lat")
     barrier = pltpu.get_barrier_semaphore()
@@ -461,30 +495,83 @@
         cells_copy(k).wait()
 
     loop(lats, begin, 1)
+
+    cells, width = lat_ref.shape
+    ch = wdk_ref.shape[0]
+    disks = disk_ref.shape[0] // ch
+    cw = ch * HEADS
+    hd = width // HEADS
+    hl = gdisk.shape[1] // disks
+    scale = 1.0 / math.sqrt(hd)
+
+    def project(i):
+        r = pl.ds(pl.multiple_of(i * CHUNK, CHUNK), CHUNK)
+        query[r, :] = mm(lat_ref[r, :], wq_ref[...]).astype(BF16)
+
+    loop(cells // CHUNK, project)
+
+    spread_ch = jnp.where(
+        lax.broadcasted_iota(jnp.int32, (cw, ch), 0) // HEADS
+        == lax.broadcasted_iota(jnp.int32, (cw, ch), 1),
+        1.0,
+        0.0,
+    ).astype(BF16)
+    head_mask = head_match(cw, width, hd)
+    bkt[...] = jnp.where(head_mask, mm(spread_ch, wdk_ref[...]), 0.0).astype(BF16)
+    bvt[...] = jnp.where(head_mask, mm(spread_ch, wdv_ref[...]), 0.0).astype(BF16)
+    sum_ch = channel_sum(cw, hl)
+    qt = mm(query[...], bkt[...], NT)
+    msum = jnp.zeros((cells, cw), F32)
+    for k in range(disks):
+        pxk = mm(disk_ref[k * ch : (k + 1) * ch, :], spread_ch, (((0,), (1,)), ((), ())))
+        px[:, k * cw : (k + 1) * cw] = pxk.astype(BF16)
+        g = jax.nn.sigmoid(mm((pxk * qt).astype(BF16), sum_ch) * scale)
+        gdisk[:, k * hl : (k + 1) * hl] = g
+        msum = msum + mm(g.astype(BF16), sum_ch, NT) * pxk
+    mdisk[...] = msum.astype(BF16)
+
     own.wait()
     own_cells.wait()
     loop(lats, end, 1)
 
 
-def send_rows(feats, cells):
+def send_rows(feats, cells, lat_flat, disk, wdk, wdv, wq):
     lats = cells.shape[0]
+    count, width = lat_flat.shape
+    ch = wdk.shape[0]
+    disks = disk.shape[0] // ch
+    cw = ch * HEADS
     dma = pltpu.SemaphoreType.DMA
     return pl.pallas_call(
         send_kernel,
         out_shape=(
             jax.ShapeDtypeStruct(feats.shape, feats.dtype),
             jax.ShapeDtypeStruct(cells.shape, cells.dtype),
+            jax.ShapeDtypeStruct((count, width), BF16),
+            jax.ShapeDtypeStruct((count, disks * cw), BF16),
+            jax.ShapeDtypeStruct((count, disks * 128), F32),
+            jax.ShapeDtypeStruct((count, cw), BF16),
+            jax.ShapeDtypeStruct((cw, width), BF16),
+            jax.ShapeDtypeStruct((cw, width), BF16),
         ),
-        in_specs=[anywhere(), anywhere()],
-        out_specs=(anywhere(), anywhere()),
+        in_specs=[anywhere(), anywhere()] + [vmem()] * 5,
+        out_specs=(anywhere(), anywhere()) + (vmem(),) * 6,
         scratch_shapes=[dma((lats,))] * 4 + [dma((2,))],
-        compiler_params=pltpu.CompilerParams(collective_id=1, has_side_effects=True),
+        compiler_params=pltpu.CompilerParams(
+            collective_id=1, has_side_effects=True, vmem_limit_bytes=60 * 1024 * 1024
+        ),
         name="send_rows",
-    )(feats, cells)
+    )(feats, cells, lat_flat, disk, wdk, wdv, wq)
+
+
+def axis_peer(v, k):
+    return lax.rem(v + k, SIDE)
 
 
 def reduce_kernel(
-    wide_a,
+    cut_a,
+    cut_b,
+    parts,
     gw_ref,
     gs_ref,
     loss_ref,
@@ -501,17 +588,28 @@
     r2a,
     s2b,
     r2b,
+    s2c,
+    r2c,
+    s3a,
+    r3a,
+    s3b,
+    r3b,
+    s3c,
+    r3c,
+    r4a,
+    r4b,
+    r4c,
     sg2,
     rg2,
-    r3a,
-    r3b,
     rg3,
     sg3,
     g4,
     t4,
     t5,
+    t6,
     mine,
     plane,
+    chips,
     local,
     s_core,
     r_core,
@@ -519,14 +617,16 @@
     r_back,
     s_a2,
     r_a2,
+    s_b2,
+    r_b2,
+    s_c2,
+    r_c2,
+    s_p3,
+    r_p3,
+    s_p4,
+    r_p4,
     s_g2,
     r_g2,
-    s_b2,
-    r_b2,
-    s_a3,
-    r_a3,
-    s_b3,
-    r_b3,
     s_g3,
     r_g3,
     s_g4,
@@ -537,163 +637,186 @@
     r_g5,
     s_t5,
     r_t5,
+    s_g6,
+    r_g6,
+    s_t6,
+    r_t6,
 ):
-    xs, cores, lats, slab, width = gw_ref.shape
+    xs, cores, ys, zs, slab, width = gw_ref.shape
     lons = xs * cores
+    lats = ys * zs
     lon = lax.axis_index("lon")
     p = lax.axis_index("lat")
     x, c = lon // cores, lon % cores
+    y, z = p // zs, p % zs
     other = 1 - c
-    rest = pl.ds(wide_a, width - wide_a)
-    first = pl.ds(0, wide_a)
+    cols_a = pl.ds(0, cut_a)
+    cols_b = pl.ds(cut_a, cut_b - cut_a)
+    cols_c = pl.ds(cut_b, width - cut_b)
     piece = g4.shape[1]
     pieces = small_ref.shape[1]
-    blocks = lats // SIDE
-
-    def to_lon(target, src, dst, ssem, rsem):
+
+    def remote(axis, target, src, dst, ssem, rsem):
         return pltpu.make_async_remote_copy(
             src_ref=src,
             dst_ref=dst,
             send_sem=ssem,
             recv_sem=rsem,
-            device_id={"lon": target},
+            device_id={axis: target},
             device_id_type=pl.DeviceIdType.MESH,
         )
 
-    def to_lat(target, src, dst, ssem, rsem):
-        return pltpu.make_async_remote_copy(
-            src_ref=src,
-            dst_ref=dst,
-            send_sem=ssem,
-            recv_sem=rsem,
-            device_id={"lat": target},
-            device_id_type=pl.DeviceIdType.MESH,
+    def to_x(k, src, dst, ssem, rsem):
+        return remote("lon", axis_peer(x, k) * cores + c, src, dst, ssem, rsem)
+
+    def to_y(k, src, dst, ssem, rsem):
+        return remote("lat", axis_peer(y, k) * zs + z, src, dst, ssem, rsem)
+
+    def to_z(k, src, dst, ssem, rsem):
+        return remote("lat", y * zs + axis_peer(z, k), src, dst, ssem, rsem)
+
+    barrier = pltpu.get_barrier_semaphore()
+
+    def greet(axis, target):
+        pl.semaphore_signal(
+            barrier, inc=1, device_id={axis: target}, device_id_type=pl.DeviceIdType.MESH
         )
 
-    def x_peer(k):
-        return lax.rem(x + k, xs)
-
-    barrier = pltpu.get_barrier_semaphore()
-
-    def greet_lat(k):
-        pl.semaphore_signal(
-            barrier, inc=1, device_id={"lat": lat_peer(p, k)}, device_id_type=pl.DeviceIdType.MESH
-        )
-
-    def greet_lon(k):
-        pl.semaphore_signal(
-            barrier, inc=1, device_id={"lon": lax.rem(lon + k, lons)}, device_id_type=pl.DeviceIdType.MESH
-        )
-
-    loop(lats, greet_lat, 1)
-    loop(lons, greet_lon, 1)
+    loop(lats, lambda k: greet("lat", lat_peer(p, k)), 1)
+    loop(xs, lambda k: greet("lon", axis_peer(x, k) * cores + c), 1)
+    greet("lon", x * cores + other)
+
+    own_small = pltpu.make_async_copy(gs_ref.at[:, c], sg1, local.at[xs])
+    own_small.start()
 
     def own_copy(j):
         return pltpu.make_async_copy(gw_ref.at[j, c], s1.at[j], local.at[j])
 
     loop(xs, lambda j: own_copy(j).start())
-    own_small = pltpu.make_async_copy(gs_ref.at[:, c], sg1, local.at[xs])
-    own_small.start()
     own_back = pltpu.make_async_copy(rgrad_ref.at[p], back_ref.at[p], local.at[xs + 1])
     own_back.start()
-    pl.semaphore_wait(barrier, lats + lons - 2)
+    pl.semaphore_wait(barrier, lats + xs - 1)
 
     mate = x * cores + other
+    core_small = remote("lon", mate, gs_ref.at[:, other], rg1, s_core.at[xs], r_core.at[xs])
+    core_small.start()
 
     def core_copy(k):
-        j = x_peer(k)
-        return to_lon(mate, gw_ref.at[j, other], r1.at[j], s_core.at[k], r_core.at[k])
-
-    core_small = to_lon(mate, gs_ref.at[:, other], rg1, s_core.at[xs], r_core.at[xs])
+        j = axis_peer(x, k)
+        return remote("lon", mate, gw_ref.at[j, other], r1.at[j], s_core.at[k], r_core.at[k])
+
     loop(xs, lambda k: core_copy(k).start(), 1)
-    core_small.start()
     core_copy(0).start()
 
     def back_copy(k):
         to = lat_peer(p, k)
-        return to_lat(to, rgrad_ref.at[to], back_ref.at[p], s_back.at[k], r_back.at[k])
-
-    loop(lats, lambda k: back_copy(k).start(), 1)
+        return remote("lat", to, rgrad_ref.at[to], back_ref.at[p], s_back.at[k], r_back.at[k])
+
+    def back_part(i):
+        loop(parts[i + 1], lambda k: back_copy(k).start(), parts[i])
+
+    back_part(0)
 
     def a2_copy(k):
-        j = x_peer(k)
-        return to_lon(
-            j * cores + c, s1.at[j, :, :, first], r2a.at[k - 1], s_a2.at[k], r_a2.at[k]
+        j = axis_peer(x, k)
+        return to_x(k, s1.at[j, :, :, :, cols_a], r2a.at[k - 1], s_a2.at[k], r_a2.at[k])
+
+    def b2_copy(k):
+        return to_y(
+            k, s1.at[:, axis_peer(y, k), :, :, cols_b], r2b.at[k - 1], s_b2.at[k], r_b2.at[k]
         )
 
+    def c2_copy(k):
+        return to_z(
+            k, s1.at[:, :, axis_peer(z, k), :, cols_c], r2c.at[k - 1], s_c2.at[k], r_c2.at[k]
+        )
+
     def g2_copy(k):
-        j = x_peer(k)
-        return to_lon(j * cores + c, sg1.at[j], rg2.at[k - 1], s_g2.at[k], r_g2.at[k])
-
-    def b2_copy(k):
-        to = lat_peer(p, k)
-        return to_lat(to, s1.at[:, to, :, rest], r2b.at[k - 1], s_b2.at[k], r_b2.at[k])
+        return to_x(k, sg1.at[axis_peer(x, k)], rg2.at[k - 1], s_g2.at[k], r_g2.at[k])
+
+    own_small.wait()
+    core_small.wait_recv()
+    sg1[...] = sg1[...] + rg1[...]
+    loop(xs, lambda k: g2_copy(k).start(), 1)
 
     def add_core(j):
         def step(i):
-            at = pl.ds(i * SIDE, SIDE)
-            s1[j, at] = s1[j, at] + r1[j, at]
-
-        loop(blocks, step)
+            s1[j, i] = s1[j, i] + r1[j, i]
+
+        loop(ys, step)
 
     def core_step(k):
-        j = x_peer(k)
+        j = axis_peer(x, k)
         own_copy(j).wait()
         core_copy(k).wait_recv()
         add_core(j)
         a2_copy(k).start()
 
     loop(xs, core_step, 1)
-    own_small.wait()
-    core_small.wait_recv()
-    sg1[...] = sg1[...] + rg1[...]
-    loop(xs, lambda k: g2_copy(k).start(), 1)
     own_copy(x).wait()
     core_copy(0).wait_recv()
     add_core(x)
-    loop(lats, lambda k: b2_copy(k).start(), 1)
-
-    loop(xs, lambda k: a2_copy(k).wait_recv(), 1)
-    loop(xs, lambda k: g2_copy(k).wait_recv(), 1)
-
-    def a3_copy(k):
-        to = lat_peer(p, k)
-        return to_lat(to, s2a.at[to], r3a.at[k - 1], s_a3.at[k], r_a3.at[k])
+
+    def spread(k):
+        b2_copy(k).start()
+        c2_copy(k).start()
+
+    loop(SIDE, spread, 1)
 
     def g3_copy(k):
         to = lat_peer(p, k)
-        return to_lat(to, sg2.at[to], rg3.at[k - 1], s_g3.at[k], r_g3.at[k])
-
-    def b3_copy(k):
-        j = x_peer(k)
-        return to_lon(j * cores + c, s2b.at[j], r3b.at[k - 1], s_b3.at[k], r_b3.at[k])
-
+        return remote("lat", to, sg2.at[to], rg3.at[k - 1], s_g3.at[k], r_g3.at[k])
+
+    loop(xs, lambda k: g2_copy(k).wait_recv(), 1)
     total = sg1[x].astype(F32)
     for k in range(xs - 1):
         total = total + rg2[k].astype(F32)
-    sg2[...] = jnp.zeros(sg2.shape, BF16)
+    sg2[pieces:] = jnp.zeros((lats - pieces,) + sg2.shape[1:], BF16)
     sg2[:pieces] = total.astype(BF16).reshape(pieces, piece, total.shape[1])
+    loop(lats, lambda k: g3_copy(k).start(), 1)
+
+    def a3_copy(k):
+        return to_y(k, s2a.at[axis_peer(y, k)], r3a.at[k - 1], s_p3.at[0, k], r_p3.at[0, k])
+
+    def b3_copy(k):
+        return to_z(k, s2b.at[:, axis_peer(z, k)], r3b.at[k - 1], s_p3.at[1, k], r_p3.at[1, k])
+
+    def c3_copy(k):
+        return to_x(k, s2c.at[axis_peer(x, k)], r3c.at[k - 1], s_p3.at[2, k], r_p3.at[2, k])
+
+    loop(SIDE, lambda k: a2_copy(k).wait_recv(), 1)
 
     def sum_a(i):
-        value = s1[x, i, :, :wide_a].astype(F32)
-        for k in range(xs - 1):
+        value = s1[x, i, :, :, :cut_a].astype(F32)
+        for k in range(SIDE - 1):
             value = value + r2a[k, i].astype(F32)
         s2a[i] = value.astype(BF16)
 
-    loop(lats, sum_a)
-    loop(lats, lambda k: a3_copy(k).start(), 1)
-    loop(lats, lambda k: g3_copy(k).start(), 1)
-    loop(lats, lambda k: b2_copy(k).wait_recv(), 1)
-
-    def sum_b(j):
-        def add(k, value):
-            return value + r2b[k, j].astype(F32)
-
-        s2b[j] = lax.fori_loop(0, lats - 1, add, s1[j, p, :, wide_a:].astype(F32)).astype(BF16)
+    loop(ys, sum_a)
+    loop(SIDE, lambda k: a3_copy(k).start(), 1)
+
+    loop(SIDE, lambda k: c2_copy(k).wait_recv(), 1)
+
+    def sum_c(i):
+        value = s1[i, :, z, :, cut_b:].astype(F32)
+        for k in range(SIDE - 1):
+            value = value + r2c[k, i].astype(F32)
+        s2c[i] = value.astype(BF16)
+
+    loop(xs, sum_c)
+    loop(SIDE, lambda k: c3_copy(k).start(), 1)
+    loop(SIDE, lambda k: b2_copy(k).wait_recv(), 1)
+
+    def sum_b(i):
+        value = s1[i, y, :, :, cut_a:cut_b].astype(F32)
+        for k in range(SIDE - 1):
+            value = value + r2b[k, i].astype(F32)
+        s2b[i] = value.astype(BF16)
 
     loop(xs, sum_b)
-    loop(xs, lambda k: b3_copy(k).start(), 1)
-
+    loop(SIDE, lambda k: b3_copy(k).start(), 1)
+
+    back_part(1)
     loop(lats, lambda k: g3_copy(k).wait_recv(), 1)
 
     def add_small(k, value):
@@ -703,21 +826,58 @@
     g4[p] = sg3[...]
 
     def g4_copy(k):
-        return to_lat(lat_peer(p, k), sg3, g4.at[p], s_g4.at[k], r_g4.at[k])
+        return remote("lat", lat_peer(p, k), sg3, g4.at[p], s_g4.at[k], r_g4.at[k])
 
     loop(lats, lambda k: g4_copy(k).start(), 1)
-    loop(lats, lambda k: a3_copy(k).wait_recv(), 1)
-
-    def add_share(k, value):
-        return value + r3a[k].astype(F32)
-
-    share_a = lax.fori_loop(0, lats - 1, add_share, s2a[p].astype(F32))
-    loop(xs, lambda k: b3_copy(k).wait_recv(), 1)
-    share_b = s2b[x].astype(F32)
-    for k in range(xs - 1):
-        share_b = share_b + r3b[k].astype(F32)
-    share_ref[:, :wide_a] = share_a
-    share_ref[:, wide_a:] = share_b
+
+    def a4_copy(k):
+        return to_z(k, s3a.at[axis_peer(z, k)], r4a.at[k - 1], s_p4.at[0, k], r_p4.at[0, k])
+
+    def b4_copy(k):
+        return to_x(k, s3b.at[axis_peer(x, k)], r4b.at[k - 1], s_p4.at[1, k], r_p4.at[1, k])
+
+    def c4_copy(k):
+        return to_y(k, s3c.at[axis_peer(y, k)], r4c.at[k - 1], s_p4.at[2, k], r_p4.at[2, k])
+
+    def summed(own, others):
+        value = own.astype(F32)
+        for k in range(SIDE - 1):
+            value = value + others[k].astype(F32)
+        return value
+
+    loop(SIDE, lambda k: a3_copy(k).wait_recv(), 1)
+    s3a[...] = summed(s2a[y], r3a).astype(BF16)
+    loop(SIDE, lambda k: a4_copy(k).start(), 1)
+    loop(SIDE, lambda k: c3_copy(k).wait_recv(), 1)
+    s3c[...] = summed(s2c[x], r3c).astype(BF16)
+    loop(SIDE, lambda k: c4_copy(k).start(), 1)
+    loop(SIDE, lambda k: b3_copy(k).wait_recv(), 1)
+    s3b[...] = summed(s2b[:, z], r3b).astype(BF16)
+    loop(SIDE, lambda k: b4_copy(k).start(), 1)
+    back_part(2)
+
+    def g5_copy(k):
+        return to_x(
+            k, g4.at[pl.ds(0, pieces)], small_ref.at[lon], s_g5.at[k], r_g5.at[k]
+        )
+
+    def g6_copy(j):
+        at = j * cores + c
+        return remote("lon", mate, small_ref.at[at], small_ref.at[at], s_g6.at[j], r_g6.at[j])
+
+    loop(lats, lambda k: g4_copy(k).wait_recv(), 1)
+    small_ref[lon] = g4[:pieces]
+    loop(SIDE, lambda k: g5_copy(k).start(), 1)
+
+    loop(SIDE, lambda k: a4_copy(k).wait_recv(), 1)
+    share_a = summed(s3a[z], r4a)
+    loop(SIDE, lambda k: c4_copy(k).wait_recv(), 1)
+    share_c = summed(s3c[y], r4c)
+    loop(SIDE, lambda k: b4_copy(k).wait_recv(), 1)
+    share_b = summed(s3b[x], r4b)
+    share_ref[:, :cut_a] = share_a
+    share_ref[:, cut_a:cut_b] = share_b
+    share_ref[:, cut_b:] = share_c
     half = slab // 2
 
     def lane_sums(value):
@@ -727,7 +887,7 @@
             total = total + value[:, j * 128 : (j + 1) * 128]
         return total
 
-    square = jnp.concatenate([share_a * share_a, share_b * share_b], axis=1)
+    square = jnp.concatenate([share_a * share_a, share_b * share_b, share_c * share_c], axis=1)
     row = lax.broadcasted_iota(jnp.int32, mine.shape, 0)
     mine[...] = jnp.where(
         row == 0,
@@ -740,111 +900,143 @@
     )
 
     def t4_copy(k):
-        return to_lat(lat_peer(p, k), mine, t4.at[k - 1], s_t4.at[k], r_t4.at[k])
+        return remote("lat", lat_peer(p, k), mine, t4.at[k - 1], s_t4.at[k], r_t4.at[k])
 
     loop(lats, lambda k: t4_copy(k).start(), 1)
-
-    loop(lats, lambda k: g4_copy(k).wait_recv(), 1)
-
-    def g5_copy(k):
-        return to_lon(
-            lax.rem(lon + k, lons), g4.at[pl.ds(0, pieces)], small_ref.at[lon], s_g5.at[k], r_g5.at[k]
-        )
-
-    loop(lons, lambda k: g5_copy(k).start(), 1)
-    small_ref[lon] = g4[:pieces]
+    back_part(3)
+    loop(SIDE, lambda k: g5_copy(k).wait_recv(), 1)
+    loop(xs, lambda j: g6_copy(j).start())
+
+    loop(xs, lambda k: core_copy(k).wait_send())
+    core_small.wait_send()
+
+    def sent_side(k):
+        a2_copy(k).wait_send()
+        g2_copy(k).wait_send()
+        b2_copy(k).wait_send()
+        c2_copy(k).wait_send()
+        a3_copy(k).wait_send()
+        b3_copy(k).wait_send()
+        c3_copy(k).wait_send()
+        a4_copy(k).wait_send()
+        b4_copy(k).wait_send()
+        c4_copy(k).wait_send()
+
+    loop(SIDE, sent_side, 1)
+
     loop(lats, lambda k: t4_copy(k).wait_recv(), 1)
     plane[...] = lax.fori_loop(0, lats - 1, lambda k, value: value + t4[k], mine[...])
 
     def t5_copy(k):
-        return to_lon(lax.rem(lon + k, lons), plane, t5.at[k - 1], s_t5.at[k], r_t5.at[k])
-
-    loop(lons, lambda k: t5_copy(k).start(), 1)
-    loop(lons, lambda k: t5_copy(k).wait_recv(), 1)
-    stat_ref[...] = lax.fori_loop(0, lons - 1, lambda k, value: value + t5[k], plane[...])
-    loop(lons, lambda k: g5_copy(k).wait_recv(), 1)
-    own_back.wait()
-    loop(lats, lambda k: back_copy(k).wait_recv(), 1)
-
-    loop(xs, lambda k: core_copy(k).wait_send())
-    core_small.wait_send()
-
-    def sent_x(k):
-        a2_copy(k).wait_send()
-        g2_copy(k).wait_send()
-        b3_copy(k).wait_send()
-
-    loop(xs, sent_x, 1)
+        return to_x(k, plane, t5.at[k - 1], s_t5.at[k], r_t5.at[k])
+
+    loop(SIDE, lambda k: t5_copy(k).start(), 1)
+    loop(SIDE, lambda k: t5_copy(k).wait_recv(), 1)
+    chips[...] = summed(plane[...], t5)
+    t6_copy = remote("lon", mate, chips, t6, s_t6.at[0], r_t6.at[0])
+    t6_copy.start()
 
     def sent_lat(k):
-        back_copy(k).wait_send()
-        b2_copy(k).wait_send()
-        a3_copy(k).wait_send()
+        back_copy(k).wait()
         g3_copy(k).wait_send()
         g4_copy(k).wait_send()
         t4_copy(k).wait_send()
 
     loop(lats, sent_lat, 1)
-
-    def sent_lon(k):
+    own_back.wait()
+    loop(xs, lambda j: g6_copy(j).wait())
+
+    def sent_x(k):
         g5_copy(k).wait_send()
         t5_copy(k).wait_send()
 
-    loop(lons, sent_lon, 1)
+    loop(SIDE, sent_x, 1)
+    t6_copy.wait()
+    stat_ref[...] = chips[...] + t6[...]
 
 
 def reduce_all(gw, gs, loss, rgrad):
     xs, cores, lats, slab, width = gw.shape
+    ys, zs = lats // SIDE, SIDE
     lons = xs * cores
     small_rows = gs.shape[2]
     piece = 32
     pieces = small_rows // piece
-    wide_a = 640
-    wide_b = width - wide_a
+    cut_a, cut_b = 384, 768
+    parts = (1, lats, lats, lats, lats)
+    wa, wb, wc = cut_a, cut_b - cut_a, width - cut_b
     dma = pltpu.SemaphoreType.DMA
 
     def buf(*shape, dtype=BF16):
         return pltpu.VMEM(shape, dtype)
 
-    pairs = [xs + 1, lats, xs, xs, lats, lats, xs, lats, lats, lats, lons, lons]
+    pairs = [
+        (xs + 1,),
+        (lats,),
+        (SIDE,),
+        (SIDE,),
+        (SIDE,),
+        (3, SIDE),
+        (3, SIDE),
+        (SIDE,),
+        (lats,),
+        (lats,),
+        (lats,),
+        (SIDE,),
+        (SIDE,),
+        (xs,),
+        (1,),
+    ]
+    n = SIDE - 1
     return pl.pallas_call(
-        functools.partial(reduce_kernel, wide_a),
+        functools.partial(reduce_kernel, cut_a, cut_b, parts),
         out_shape=(
             jax.ShapeDtypeStruct((slab, width), F32),
             jax.ShapeDtypeStruct((lons, pieces, piece, 128), BF16),
             jax.ShapeDtypeStruct((8, 128), F32),
             jax.ShapeDtypeStruct(rgrad.shape, BF16),
         ),
-        in_specs=[anywhere(), vmem(), vmem(), anywhere()],
+        in_specs=[anywhere(), anywhere(), vmem(), anywhere()],
         out_specs=(vmem(), vmem(), vmem(), anywhere()),
         scratch_shapes=[
-            buf(xs, lats, slab, width),
-            buf(xs, lats, slab, width),
+            buf(xs, ys, zs, slab, width),
+            buf(xs, ys, zs, slab, width),
             buf(xs, small_rows, 128),
             buf(xs, small_rows, 128),
-            buf(lats, slab, wide_a),
-            buf(xs - 1, lats, slab, wide_a),
-            buf(xs, slab, wide_b),
-            buf(lats - 1, xs, slab, wide_b),
+            buf(ys, zs, slab, wa),
+            buf(n, ys, zs, slab, wa),
+            buf(xs, zs, slab, wb),
+            buf(n, xs, zs, slab, wb),
+            buf(xs, ys, slab, wc),
+            buf(n, xs, ys, slab, wc),
+            buf(zs, slab, wa),
+            buf(n, zs, slab, wa),
+            buf(xs, slab, wb),
+            buf(n, xs, slab, wb),
+            buf(ys, slab, wc),
+            buf(n, ys, slab, wc),
+            buf(n, slab, wa),
+            buf(n, slab, wb),
+            buf(n, slab, wc),
             buf(lats, piece, 128),
             buf(xs - 1, small_rows, 128),
-            buf(lats - 1, slab, wide_a),
-            buf(xs - 1, slab, wide_b),
             buf(lats - 1, piece, 128),
             buf(piece, 128),
             buf(lats, piece, 128),
             buf(lats - 1, 8, 128, dtype=F32),
-            buf(lons - 1, 8, 128, dtype=F32),
+            buf(n, 8, 128, dtype=F32),
+            buf(8, 128, dtype=F32),
+            buf(8, 128, dtype=F32),
             buf(8, 128, dtype=F32),
             buf(8, 128, dtype=F32),
             dma((xs + 2,)),
         ]
-        + [dma((n,)) for n in pairs for _ in range(2)],
+        + [dma(n) for n in pairs for _ in range(2)],
         compiler_params=pltpu.CompilerParams(
-            collective_id=2, has_side_effects=True, vmem_limit_bytes=40 * 1024 * 1024
+            collective_id=2, has_side_effects=True, vmem_limit_bytes=60 * 1024 * 1024
         ),
         name="reduce_all",
-    )(gw, gs, loss, rgrad)
+    )(gw.reshape((xs, cores, ys, zs, slab, width)), gs, loss, rgrad)
 
 
 def finish_kernel(
@@ -947,20 +1139,27 @@
     feat = radiances.shape[1]
     ch = w_disk_key.shape[0]
     sfeats, scells, slot = pack(block_tile, block_rows, radiances, row_cells, lat_count)
-    got_feats, got_cells = send_rows(sfeats.reshape(lat_count, -1, feat), scells)
-    weight = jnp.asarray(cell_weights(tile_lat * lat_count))
+    lat_flat = latents.reshape(cells, width)
+    got_feats, got_cells, *disk_state = send_rows(
+        sfeats.reshape(lat_count, -1, feat),
+        scells,
+        lat_flat,
+        disk_pixels.reshape(-1, cells),
+        w_disk_key,
+        w_disk_value,
+        w_query,
+    )
     lgrad, rgrad, gw, gs, loss = tile_step(
         device_count,
-        weight,
+        jnp.asarray(cell_weights(tile_lat * lat_count)),
         got_feats.reshape(-1, feat),
         got_cells,
-        latents.reshape(cells, width),
-        disk_pixels.reshape(-1, cells),
+        lat_flat,
+        disk_state,
+        w_key,
+        w_value,
         targets.reshape(cells, out_width),
         w_query,
-        jnp.concatenate([w_key, w_value], axis=1),
-        w_disk_key,
-        w_disk_value,
         w_out,
         w_decode,
     )

time: 148 us -> 142 us (0.959)
  Pallas kernels: 138 us -> 136 us
  other arithmetic: 1.86 us -> 0 us
    pallas_call x1, Pallas kernels: 62.1 us -> 36.7 us  [tile_step(): pl.pallas_call(tile_kernel, out_shape=(jax.ShapeDtypeStruct((cell_count,...]
    pallas_call x1, Pallas kernels: 49.4 us -> 68.5 us  [reduce_all(): pl.pallas_call(functools.partial(reduce_kernel, cut_a, cut_b, parts), out...]
    pallas_call x1, Pallas kernels: 22.6 us -> 26.5 us  [send_rows(): pl.pallas_call(send_kernel, out_shape=(jax.ShapeDtypeStruct(feats.shape,...]
    concatenate x1 -> x0, other arithmetic: 1.86 us -> none  [body(): jnp.concatenate([w_key, w_value], axis=1)]
where the time goes in v3:
time: 142 us
  Pallas kernels  136 us (96%)
  local copies, waits for them, and re-layouts  5.34 us (4%)
    pallas_call x1, Pallas kernels, reduce_all(): pl.pallas_call(functools.partial(reduce_kernel, cut_a, cut_b, parts), out...  68.5 us
    pallas_call x1, Pallas kernels, tile_step(): pl.pallas_call(tile_kernel, out_shape=(jax.ShapeDtypeStruct((cell_count,...  36.7 us
    pallas_call x1, Pallas kernels, send_rows(): pl.pallas_call(send_kernel, out_shape=(jax.ShapeDtypeStruct(feats.shape,...  26.5 us
    unnamed x11, local copies, waits for them, and re-layouts  5.34 us

profile of v3, /device:TPU:1, one launch (start us, length us, event | category | flops | bytes accessed | tf_op | source)
XLA Modules:
  0.0 141.8 jit_solution(6433269382736428022)
XLA Ops:
  0.6 1.5 %copy.26 = bf16[10,8,4,128]{3,1,2,0:T(8,128)(2,1)} copy(bf16[10,8,4,128]{3,2,1,0:T(4,128)(2,1)} %bitcast.26) | data formatting | bytes 163840
  2.2 2.1 %pack.1 = (bf16[4096,128]{1,0:T(8,128)(2,1)}, s32[16,8,128]{2,1,0:T(8,128)}, s32[16]{0:T(128)}) custom-call(s32[16]{0:T(128)} %tile_ref.1, s32[16]{0:T(128)} %rows_ref.1, bf16[2048,128]{1,0:T(8,128)(2,1)} %feats_ref.1, s32[16,128]{1,0:T(8,128)} %bitcast.27), custom_call_target="tpu_custom_call" | custom-call | tf_op jit(solution)/shard_map/pack/pallas_call | solution.py:79
  4.3 26.5 %send_rows.1 = (bf16[16,256,128]{2,1,0:T(8,128)(2,1)}, s32[16,8,128]{2,1,0:T(8,128)}, bf16[512,1024]{1,0:T(8,128)(2,1)}, bf16[512,1280]{1,0:T(8,128)(2,1)}, f32[...) custom-call(bf16[16,256,128]{2,1,0:T(8,128)(2,1)} %bitcast.22, ...), custom_call_target="tpu_custom_call" | custom-call | tf_op jit(solution)/shard_map/send_rows/pallas_call | solution.py:545
  30.8 36.7 %tile.1 = (f32[512,1024]{1,0:T(8,128)}, bf16[4096,128]{1,0:T(8,128)(2,1)}, bf16[128,16,1024]{2,1,0:T(8,128)(2,1)}, bf16[8,288,128]{2,1,0:T(8,128)(2,1)}, f32[8,128]{1,0:T(8,128)}) custom-call(f32[64]{0:T(128)} %constant.2.clone.weight_ref, bf16[4096,128]{1,0:T(8,128)(2,1)} %bitcast.21, s32[16,8,128]{2,1,0:T(8,128)} %get-tuple-element.41.cells_ref, ...), custom_call_target="tpu_custom_call" | custom-call | tf_op jit(solution)/shard_map/tile/pallas_call | solution.py:369
  67.5 0.0 copy-start.4
  67.5 68.5 %reduce_all.1 = (f32[16,1024]{1,0:T(8,128)}, bf16[8,9,32,128]{3,2,1,0:T(8,128)(2,1)}, f32[8,128]{1,0:T(8,128)}, bf16[16,256,128]{2,1,0:T(8,128)(2,1)}) custom-call(bf16[4,2,4,4,16,1024]{5,4,3,2,1,0:T(8,128)(2,1)} %bitcast.17, bf16[4,2,288,128]{3,2,1,0:T(8,128)(2,1)} %bitcast.23, f32[8,128]{1,0:T(8,128)} %get-tuple-element.50.loss_ref, ...), custom_call_target="tpu_custom_call" | custom-call | tf_op jit(solution)/shard_map/reduce_all/pallas_call | solution.py:991
  136.0 0.0 copy-done.4
  136.0 0.0 copy-start
  136.0 1.2 copy-done
  137.3 0.0 copy-start.1
  137.3 1.1 copy-done.1
  138.3 0.0 copy-start.2
  138.3 0.8 copy-done.2
  139.2 0.0 copy-start.3
  139.2 0.7 copy-done.3
  139.8 2.0 %finish.1 = (bf16[2048,128]{1,0:T(8,128)(2,1)}, f32[8,1024]{1,0:T(8,128)}, f32[8,1024]{1,0:T(8,128)}, f32[128,1024]{1,0:T(8,128)}, f32[128,1024]{1,0:T(8,128)}, ...) custom-call(s32[16]{0:T(128)S(1)} %copy-done.4, bf16[4096,128]{1,0:T(8,128)(2,1)S(1)} %bitcast.16, ...), custom_call_target="tpu_custom_call" | custom-call | tf_op jit(solution)/shard_map/finish/pallas_call | solution.py:1101
Async XLA Ops:
  67.5 68.6 %copy-start.4 = (s32[16]{0:T(128)S(1)}, s32[16]{0:T(128)}, u32[]{:S(2)}) copy-start(s32[16]{0:T(128)} %get-tuple-element.37.slot_ref) | copy-start | bytes 196
  136.0 1.2 copy-start
  137.3 1.1 copy-start.1
  138.3 0.8 copy-start.2
  139.2 0.7 copy-start.3

commit v4 on v3

--- a/solution.py
+++ b/solution.py
@@ -12,6 +12,7 @@
 HEADS = 16
 CAP = 2
 CHUNK = 256
+ROWCHUNK = 256
 F32 = jnp.float32
 BF16 = jnp.bfloat16
 
@@ -131,6 +132,7 @@
     lgrad_ref,
     hsum,
     hspread,
+    wkv,
     countv,
     counts,
     csem,
@@ -181,6 +183,8 @@
         1.0,
         0.0,
     ).astype(BF16)
+    wkv[:, :width] = wk_ref[...]
+    wkv[:, width:] = wv_ref[...]
     comp[...] = jnp.zeros(comp.shape, BF16)
     cellb[...] = jnp.full(cellb.shape, -1, jnp.int32)
 
@@ -201,9 +205,9 @@
         comp[at, :] = jnp.where(row < counts[place(s), 0], got, jnp.zeros_like(got))
         cellb[at, :] = jnp.broadcast_to(columns[:, place(s) : place(s) + 1], (block_len, 128))
         offset = offset + ((counts[place(s), 0] + 15) // 16) * 16
-    chunk_total = (offset + (CHUNK - 1)) // CHUNK
-
-    lane = lax.broadcasted_iota(jnp.int32, (CHUNK, 128), 1)
+    chunk_total = (offset + (ROWCHUNK - 1)) // ROWCHUNK
+
+    lane = lax.broadcasted_iota(jnp.int32, (ROWCHUNK, 128), 1)
 
     def one_hot(r):
         cb = cellb[r, :]
@@ -216,20 +220,18 @@
         )
 
     def forward(i, _):
-        r = pl.ds(pl.multiple_of(i * CHUNK, CHUNK), CHUNK)
+        r = pl.ds(pl.multiple_of(i * ROWCHUNK, ROWCHUNK), ROWCHUNK)
         f = comp[r, :]
-        key = mm(f, wk_ref[...]).astype(BF16)
-        value = mm(f, wv_ref[...]).astype(BF16)
-        kv[r, :width] = key
-        kv[r, width:] = value
+        both = mm(f, wkv[...]).astype(BF16)
+        kv[r, :] = both
         oh = one_hot(r)
         q = mm(oh, query[...]).astype(BF16)
-        qr[pl.ds(pl.multiple_of(i * (CHUNK // 16), CHUNK // 16), CHUNK // 16)] = q.reshape(
-            CHUNK // 16, 16, width
+        qr[pl.ds(pl.multiple_of(i * (ROWCHUNK // 16), ROWCHUNK // 16), ROWCHUNK // 16)] = q.reshape(
+            ROWCHUNK // 16, 16, width
         )
-        g = jax.nn.sigmoid(mm(q * key, hsum[...]) * scale)
+        g = jax.nn.sigmoid(mm(q * both[:, :width], hsum[...]) * scale)
         gate[r, :] = g
-        term = mm(g.astype(BF16), hspread[...]).astype(BF16) * value
+        term = mm(g.astype(BF16), hspread[...]).astype(BF16) * both[:, width:]
         acc[...] += mm(oh, term, TN)
         return 0
 
@@ -292,7 +294,7 @@
     gkv[...] = jnp.zeros(gkv.shape, F32)
 
     def backward(i, _):
-        r = pl.ds(pl.multiple_of(i * CHUNK, CHUNK), CHUNK)
+        r = pl.ds(pl.multiple_of(i * ROWCHUNK, ROWCHUNK), ROWCHUNK)
         oh = one_hot(r)
         gm = mm(oh, gmix[...]).astype(BF16)
         g = gate[r, :]
@@ -300,11 +302,10 @@
         ds_wide = mm(ds.astype(BF16), hspread[...]).astype(BF16)
         acc[...] += mm(oh, ds_wide * kv[r, :width], TN)
         g_wide = mm(g.astype(BF16), hspread[...]).astype(BF16)
-        q = qr[pl.ds(pl.multiple_of(i * (CHUNK // 16), CHUNK // 16), CHUNK // 16)]
-        grads = jnp.concatenate([ds_wide * q.reshape(CHUNK, width), g_wide * gm], axis=1)
+        q = qr[pl.ds(pl.multiple_of(i * (ROWCHUNK // 16), ROWCHUNK // 16), ROWCHUNK // 16)]
+        grads = jnp.concatenate([ds_wide * q.reshape(ROWCHUNK, width), g_wide * gm], axis=1)
         gkv[...] += mm(comp[r, :], grads, TN)
-        back = mm(grads[:, :width], wk_ref[...], NT) + mm(grads[:, width:], wv_ref[...], NT)
-        comp[r, :] = back.astype(BF16)
+        comp[r, :] = mm(grads, wkv[...], NT).astype(BF16)
         return 0
 
     lax.fori_loop(0, chunk_total, backward, 0)
@@ -397,6 +398,7 @@
             pltpu.VMEM((cell_count, width), F32),
             pltpu.VMEM((width, 128), BF16),
             pltpu.VMEM((128, width), BF16),
+            pltpu.VMEM((feat, 2 * width), BF16),
             pltpu.VMEM((8 * sources, 128), jnp.int32),
             pltpu.SMEM((8 * sources, 128), jnp.int32),
             pltpu.SemaphoreType.DMA,
@@ -429,24 +431,31 @@
 def send_kernel(
     feats_ref,
     cells_ref,
-    lat_ref,
+    lat_hbm,
+    wq_hbm,
     disk_ref,
     wdk_ref,
     wdv_ref,
-    wq_ref,
     got_ref,
     gcells_ref,
+    query_hbm,
+    px_hbm,
+    gdisk_hbm,
+    mdisk,
+    bkt,
+    bvt,
+    lat_ref,
+    wq_ref,
     query,
     px,
     gdisk,
-    mdisk,
-    bkt,
-    bvt,
     fsend,
     frecv,
     csend,
     crecv,
     local,
+    loads,
+    stores,
 ):
     lats = cells_ref.shape[0]
     p = lax.axis_index("lat")
@@ -494,8 +503,14 @@
         feats_copy(k).wait()
         cells_copy(k).wait()
 
+    load_lat = pltpu.make_async_copy(lat_hbm, lat_ref, loads.at[0])
+    load_wq = pltpu.make_async_copy(wq_hbm, wq_ref, loads.at[1])
+    load_lat.start()
+    load_wq.start()
     loop(lats, begin, 1)
 
+    load_lat.wait()
+    load_wq.wait()
     cells, width = lat_ref.shape
     ch = wdk_ref.shape[0]
     disks = disk_ref.shape[0] // ch
@@ -509,6 +524,8 @@
         query[r, :] = mm(lat_ref[r, :], wq_ref[...]).astype(BF16)
 
     loop(cells // CHUNK, project)
+    store_query = pltpu.make_async_copy(query, query_hbm, stores.at[0])
+    store_query.start()
 
     spread_ch = jnp.where(
         lax.broadcasted_iota(jnp.int32, (cw, ch), 0) // HEADS
@@ -529,10 +546,17 @@
         gdisk[:, k * hl : (k + 1) * hl] = g
         msum = msum + mm(g.astype(BF16), sum_ch, NT) * pxk
     mdisk[...] = msum.astype(BF16)
+    store_px = pltpu.make_async_copy(px, px_hbm, stores.at[1])
+    store_px.start()
+    store_gdisk = pltpu.make_async_copy(gdisk, gdisk_hbm, stores.at[2])
+    store_gdisk.start()
 
     own.wait()
     own_cells.wait()
     loop(lats, end, 1)
+    store_query.wait()
+    store_px.wait()
+    store_gdisk.wait()
 
 
 def send_rows(feats, cells, lat_flat, disk, wdk, wdv, wq):
@@ -554,14 +578,22 @@
             jax.ShapeDtypeStruct((cw, width), BF16),
             jax.ShapeDtypeStruct((cw, width), BF16),
         ),
-        in_specs=[anywhere(), anywhere()] + [vmem()] * 5,
-        out_specs=(anywhere(), anywhere()) + (vmem(),) * 6,
-        scratch_shapes=[dma((lats,))] * 4 + [dma((2,))],
+        in_specs=[anywhere()] * 4 + [vmem()] * 3,
+        out_specs=(anywhere(),) * 5 + (vmem(),) * 3,
+        scratch_shapes=[
+            pltpu.VMEM((count, width), BF16),
+            pltpu.VMEM((width, width), BF16),
+            pltpu.VMEM((count, width), BF16),
+            pltpu.VMEM((count, disks * cw), BF16),
+            pltpu.VMEM((count, disks * 128), F32),
+        ]
+        + [dma((lats,))] * 4
+        + [dma((2,)), dma((2,)), dma((3,))],
         compiler_params=pltpu.CompilerParams(
             collective_id=1, has_side_effects=True, vmem_limit_bytes=60 * 1024 * 1024
         ),
         name="send_rows",
-    )(feats, cells, lat_flat, disk, wdk, wdv, wq)
+    )(feats, cells, lat_flat, wq, disk, wdk, wdv)
 
 
 def axis_peer(v, k):
@@ -962,7 +994,7 @@
     small_rows = gs.shape[2]
     piece = 32
     pieces = small_rows // piece
-    cut_a, cut_b = 384, 768
+    cut_a, cut_b = 512, 768
     parts = (1, lats, lats, lats, lats)
     wa, wb, wc = cut_a, cut_b - cut_a, width - cut_b
     dma = pltpu.SemaphoreType.DMA
@@ -1103,7 +1135,7 @@
         out_shape=tuple(jax.ShapeDtypeStruct(s, d) for s, d in shapes),
         in_specs=[smem()] + [vmem()] * 4,
         out_specs=(vmem(),) * len(shapes),
-        compiler_params=pltpu.CompilerParams(vmem_limit_bytes=32 * 1024 * 1024),
+        compiler_params=pltpu.CompilerParams(vmem_limit_bytes=60 * 1024 * 1024),
         name="finish",
     )(slots, got, share, small, stat)
 

time: 142 us -> 130 us (0.915)
  Pallas kernels: 136 us -> 128 us
  local copies, waits for them, and re-layouts: 5.34 us -> 1.53 us
    pallas_call x1, Pallas kernels: 68.5 us -> 63.8 us  [reduce_all(): pl.pallas_call(functools.partial(reduce_kernel, cut_a, cut_b, parts), out...]
    unnamed x11 -> x1, local copies, waits for them, and re-layouts: 5.34 us -> 1.53 us
    pallas_call x1, Pallas kernels: 26.5 us -> 24.2 us  [send_rows(): pl.pallas_call(send_kernel, out_shape=(jax.ShapeDtypeStruct(feats.shape,...]
where the time goes in v4:
time: 130 us; the launch traced here: 131 us
  Pallas kernels  128 us (98%)
  local copies, waits for them, and re-layouts  1.53 us (1%)
    pallas_call x1, Pallas kernels, reduce_all(): pl.pallas_call(functools.partial(reduce_kernel, cut_a, cut_b, parts), out...  63.8 us
    pallas_call x1, Pallas kernels, tile_step(): pl.pallas_call(tile_kernel, out_shape=(jax.ShapeDtypeStruct((cell_count,...  35.3 us
    pallas_call x1, Pallas kernels, send_rows(): pl.pallas_call(send_kernel, out_shape=(jax.ShapeDtypeStruct(feats.shape,...  24.2 us
    pallas_call x1, Pallas kernels, finish(): pl.pallas_call(functools.partial(finish_kernel, loss_scale), out_shape=tu...  2.87 us

profile of v4, /device:TPU:1, one launch (start us, length us, event | category | flops | bytes accessed | tf_op | source)
XLA Modules:
  0.0 130.5 jit_solution(16384524650320998016)
XLA Ops:
  0.6 1.5 %copy.26 = bf16[10,8,4,128]{3,1,2,0:T(8,128)(2,1)} copy(bf16[10,8,4,128]{3,2,1,0:T(4,128)(2,1)} %bitcast.26) | data formatting | bytes 163840
  2.2 2.1 %pack.1 = (bf16[4096,128]{1,0:T(8,128)(2,1)}, s32[16,8,128]{2,1,0:T(8,128)}, s32[16]{0:T(128)}) custom-call(s32[16]{0:T(128)} %tile_ref.1, s32[16]{0:T(128)} %rows_ref.1, bf16[2048,128]{1,0:T(8,128)(2,1)} %feats_ref.1, s32[16,128]{1,0:T(8,128)} %bitcast.27), custom_call_target="tpu_custom_call" | custom-call | tf_op jit(solution)/shard_map/pack/pallas_call | solution.py:80
  4.3 24.2 %send_rows.1 = (bf16[16,256,128]{2,1,0:T(8,128)(2,1)}, s32[16,8,128]{2,1,0:T(8,128)}, bf16[512,1024]{1,0:T(8,128)(2,1)}, bf16[512,1280]{1,0:T(8,128)(2,1)}, f32[...) custom-call(bf16[16,256,128]{2,1,0:T(8,128)(2,1)} %bitcast.22, ...), custom_call_target="tpu_custom_call" | custom-call | tf_op jit(solution)/shard_map/send_rows/pallas_call | solution.py:569
  28.5 35.3 %tile.1 = (f32[512,1024]{1,0:T(8,128)}, bf16[4096,128]{1,0:T(8,128)(2,1)}, bf16[128,16,1024]{2,1,0:T(8,128)(2,1)}, bf16[8,288,128]{2,1,0:T(8,128)(2,1)}, f32[8,128]{1,0:T(8,128)}) custom-call(f32[64]{0:T(128)} %constant.2.clone.weight_ref, bf16[4096,128]{1,0:T(8,128)(2,1)} %bitcast.20, s32[16,8,128]{2,1,0:T(8,128)} %get-tuple-element.41.cells_ref, ...), custom_call_target="tpu_custom_call" | custom-call | tf_op jit(solution)/shard_map/tile/pallas_call | solution.py:370
  63.8 63.8 %reduce_all.1 = (f32[16,1024]{1,0:T(8,128)}, bf16[8,9,32,128]{3,2,1,0:T(8,128)(2,1)}, f32[8,128]{1,0:T(8,128)}, bf16[16,256,128]{2,1,0:T(8,128)(2,1)}) custom-call(bf16[4,2,4,4,16,1024]{5,4,3,2,1,0:T(8,128)(2,1)} %bitcast.16, bf16[4,2,288,128]{3,2,1,0:T(8,128)(2,1)} %bitcast.23, f32[8,128]{1,0:T(8,128)} %get-tuple-element.50.loss_ref, ...), custom_call_target="tpu_custom_call" | custom-call | tf_op jit(solution)/shard_map/reduce_all/pallas_call | solution.py:1023
  127.6 2.9 %finish.1 = (bf16[2048,128]{1,0:T(8,128)(2,1)}, f32[8,1024]{1,0:T(8,128)}, f32[8,1024]{1,0:T(8,128)}, f32[128,1024]{1,0:T(8,128)}, f32[128,1024]{1,0:T(8,128)}, ...) custom-call(s32[16]{0:T(128)} %get-tuple-element.37.slot_ref, bf16[4096,128]{1,0:T(8,128)(2,1)} %bitcast.21, ...), custom_call_target="tpu_custom_call" | custom-call | tf_op jit(solution)/shard_map/finish/pallas_call | solution.py:1133

commit v5 on v4

--- a/solution.py
+++ b/solution.py
@@ -95,10 +95,10 @@
     weight_ref,
     feats_ref,
     cells_ref,
-    lat_ref,
+    lat_hbm,
     query,
-    px,
-    gdisk,
+    px_hbm,
+    gdisk_hbm,
     mdisk,
     bkt,
     bvt,
@@ -125,6 +125,9 @@
     gul,
     gmix,
     ndisk,
+    lat_ref,
+    px,
+    gdisk,
     target_ref,
     wq_ref,
     wo_ref,
@@ -159,7 +162,15 @@
     loads = [
         pltpu.make_async_copy(hbm, held, isem.at[i])
         for i, (hbm, held) in enumerate(
-            ((wo_hbm, wo_ref), (wd_hbm, wd_ref), (target_hbm, target_ref), (wq_hbm, wq_ref))
+            (
+                (wo_hbm, wo_ref),
+                (wd_hbm, wd_ref),
+                (target_hbm, target_ref),
+                (lat_hbm, lat_ref),
+                (px_hbm, px),
+                (gdisk_hbm, gdisk),
+                (wq_hbm, wq_ref),
+            )
         )
     ]
     for load in loads:
@@ -219,6 +230,11 @@
             axis=1,
         )
 
+    def one_hot_t(r):
+        row = jnp.transpose(cellb[r, :].astype(F32))[0:1, :]
+        line = lax.broadcasted_iota(jnp.int32, (cells, ROWCHUNK), 0).astype(F32)
+        return jnp.where(row == line, 1.0, 0.0).astype(BF16)
+
     def forward(i, _):
         r = pl.ds(pl.multiple_of(i * ROWCHUNK, ROWCHUNK), ROWCHUNK)
         f = comp[r, :]
@@ -232,7 +248,7 @@
         g = jax.nn.sigmoid(mm(q * both[:, :width], hsum[...]) * scale)
         gate[r, :] = g
         term = mm(g.astype(BF16), hspread[...]).astype(BF16) * both[:, width:]
-        acc[...] += mm(oh, term, TN)
+        acc[...] += mm(one_hot_t(r), term)
         return 0
 
     lax.fori_loop(0, chunk_total, forward, 0)
@@ -240,7 +256,7 @@
     lat_at = lax.axis_index("lat") * grid_rows
     tile = CHUNK
     lines = tile // 128
-    for load in loads[:3]:
+    for load in loads[:4]:
         load.wait()
 
     def middle(i, loss):
@@ -262,6 +278,8 @@
 
     loss_ref[...] = lax.fori_loop(0, cells // tile, middle, jnp.zeros((8, out_width), F32))
 
+    loads[4].wait()
+    loads[5].wait()
     head_mask = head_match(cw, width, hd)
     sum_ch = channel_sum(cw, hl)
     gt = mm(gmix[...], bvt[...], NT)
@@ -300,7 +318,7 @@
         g = gate[r, :]
         ds = mm(gm * kv[r, width:], hsum[...]) * g * (1.0 - g) * scale
         ds_wide = mm(ds.astype(BF16), hspread[...]).astype(BF16)
-        acc[...] += mm(oh, ds_wide * kv[r, :width], TN)
+        acc[...] += mm(one_hot_t(r), ds_wide * kv[r, :width])
         g_wide = mm(g.astype(BF16), hspread[...]).astype(BF16)
         q = qr[pl.ds(pl.multiple_of(i * (ROWCHUNK // 16), ROWCHUNK // 16), ROWCHUNK // 16)]
         grads = jnp.concatenate([ds_wide * q.reshape(ROWCHUNK, width), g_wide * gm], axis=1)
@@ -321,7 +339,7 @@
         )
         offset = offset + ((counts[place(s), 0] + 15) // 16) * 16
 
-    loads[3].wait()
+    loads[6].wait()
 
     def lgrad_copy(i):
         r = pl.ds(pl.multiple_of(i * tile, tile), tile)
@@ -376,7 +394,10 @@
             jax.ShapeDtypeStruct((width // 128, 2 * feat + 2 * ch, 128), BF16),
             jax.ShapeDtypeStruct((8, target.shape[1]), F32),
         ),
-        in_specs=[smem()] + [vmem()] * 11 + [anywhere()] * 4,
+        in_specs=[smem(), vmem(), vmem(), anywhere(), vmem()]
+        + [anywhere()] * 2
+        + [vmem()] * 5
+        + [anywhere()] * 4,
         out_specs=(anywhere(), vmem(), anywhere(), vmem(), vmem()),
         scratch_shapes=[
             pltpu.VMEM((rows, feat), BF16),
@@ -391,6 +412,9 @@
             pltpu.VMEM((cell_count, width), BF16),
             pltpu.VMEM((cell_count, width), BF16),
             pltpu.VMEM((cell_count, cw), BF16),
+            pltpu.VMEM(lat_flat.shape, BF16),
+            pltpu.VMEM(disk_state[1].shape, BF16),
+            pltpu.VMEM(disk_state[2].shape, F32),
             pltpu.VMEM(target.shape, F32),
             pltpu.VMEM(wq.shape, BF16),
             pltpu.VMEM(wo.shape, BF16),
@@ -403,7 +427,7 @@
             pltpu.SMEM((8 * sources, 128), jnp.int32),
             pltpu.SemaphoreType.DMA,
             pltpu.SemaphoreType.DMA((width // CHUNK,)),
-            pltpu.SemaphoreType.DMA((4,)),
+            pltpu.SemaphoreType.DMA((7,)),
             pltpu.SemaphoreType.DMA((cell_count // CHUNK,)),
         ],
         compiler_params=pltpu.CompilerParams(vmem_limit_bytes=62 * 1024 * 1024),

time: 130 us -> 129 us (level)
  no operation moved by 1% of the time
where the time goes in v5:
time: 129 us; the launch traced here: 130 us
  Pallas kernels  127 us (98%)
  local copies, waits for them, and re-layouts  1.53 us (1%)
    pallas_call x1, Pallas kernels, reduce_all(): pl.pallas_call(functools.partial(reduce_kernel, cut_a, cut_b, parts), out...  64.1 us
    pallas_call x1, Pallas kernels, tile_step(): pl.pallas_call(tile_kernel, out_shape=(jax.ShapeDtypeStruct((cell_count,...  34.2 us
    pallas_call x1, Pallas kernels, send_rows(): pl.pallas_call(send_kernel, out_shape=(jax.ShapeDtypeStruct(feats.shape,...  24.2 us
    pallas_call x1, Pallas kernels, finish(): pl.pallas_call(functools.partial(finish_kernel, loss_scale), out_shape=tu...  2.87 us

profile of v5, /device:TPU:1, one launch (start us, length us, event | category | flops | bytes accessed | tf_op | source)
XLA Modules:
  0.0 129.7 jit_solution(13733597114375478856)
XLA Ops:
  0.6 1.5 %copy.26 = bf16[10,8,4,128]{3,1,2,0:T(8,128)(2,1)} copy(bf16[10,8,4,128]{3,2,1,0:T(4,128)(2,1)} %bitcast.26) | data formatting | bytes 163840
  2.2 2.1 %pack.1 = (bf16[4096,128]{1,0:T(8,128)(2,1)}, s32[16,8,128]{2,1,0:T(8,128)}, s32[16]{0:T(128)}) custom-call(s32[16]{0:T(128)} %tile_ref.1, s32[16]{0:T(128)} %rows_ref.1, bf16[2048,128]{1,0:T(8,128)(2,1)} %feats_ref.1, s32[16,128]{1,0:T(8,128)} %bitcast.27), custom_call_target="tpu_custom_call" | custom-call | tf_op jit(solution)/shard_map/pack/pallas_call | solution.py:80
  4.3 24.2 %send_rows.1 = (bf16[16,256,128]{2,1,0:T(8,128)(2,1)}, s32[16,8,128]{2,1,0:T(8,128)}, bf16[512,1024]{1,0:T(8,128)(2,1)}, bf16[512,1280]{1,0:T(8,128)(2,1)}, f32[...) custom-call(bf16[16,256,128]{2,1,0:T(8,128)(2,1)} %bitcast.22, ...), custom_call_target="tpu_custom_call" | custom-call | tf_op jit(solution)/shard_map/send_rows/pallas_call | solution.py:593
  28.5 34.2 %tile.1 = (f32[512,1024]{1,0:T(8,128)}, bf16[4096,128]{1,0:T(8,128)(2,1)}, bf16[128,16,1024]{2,1,0:T(8,128)(2,1)}, bf16[8,288,128]{2,1,0:T(8,128)(2,1)}, f32[8,128]{1,0:T(8,128)}) custom-call(f32[64]{0:T(128)} %constant.2.clone.weight_ref, bf16[4096,128]{1,0:T(8,128)(2,1)} %bitcast.20, s32[16,8,128]{2,1,0:T(8,128)} %get-tuple-element.41.cells_ref, ...), custom_call_target="tpu_custom_call" | custom-call | tf_op jit(solution)/shard_map/tile/pallas_call | solution.py:388
  62.7 64.1 %reduce_all.1 = (f32[16,1024]{1,0:T(8,128)}, bf16[8,9,32,128]{3,2,1,0:T(8,128)(2,1)}, f32[8,128]{1,0:T(8,128)}, bf16[16,256,128]{2,1,0:T(8,128)(2,1)}) custom-call(bf16[4,2,4,4,16,1024]{5,4,3,2,1,0:T(8,128)(2,1)} %bitcast.16, bf16[4,2,288,128]{3,2,1,0:T(8,128)(2,1)} %bitcast.23, f32[8,128]{1,0:T(8,128)} %get-tuple-element.50.loss_ref, ...), custom_call_target="tpu_custom_call" | custom-call | tf_op jit(solution)/shard_map/reduce_all/pallas_call | solution.py:1047
  126.8 2.9 %finish.1 = (bf16[2048,128]{1,0:T(8,128)(2,1)}, f32[8,1024]{1,0:T(8,128)}, f32[8,1024]{1,0:T(8,128)}, f32[128,1024]{1,0:T(8,128)}, f32[128,1024]{1,0:T(8,128)}, ...) custom-call(s32[16]{0:T(128)} %get-tuple-element.37.slot_ref, bf16[4096,128]{1,0:T(8,128)(2,1)} %bitcast.21, ...), custom_call_target="tpu_custom_call" | custom-call | tf_op jit(solution)/shard_map/finish/pallas_call | solution.py:1157
